TPU v7x, 512 devices: a whole 4x8x8 slice. The times are simulated.
512 devices in a mesh: dp: 16 (over y_hi, x, core), tensor: 32 (over z, y_lo).
Axes of the slice: x: 4, y: 8 (y_hi: 2, y_lo: 4; y = y_hi * 4 + y_lo), z: 8, core: 2. Of those that a mesh axis runs over, the one named last changes fastest.
Arguments:
- drafts: bfloat16 [768, 8192], P('tensor', 'dp'), may hold values from -6 to 6
- gate_codes: bfloat16 [8192, 28672], P('dp', 'tensor'), may hold values from -8 to 7, as said below
- gate_scales: float32 [64, 28672], P('dp', 'tensor'), may hold values from 0.0012 to 0.0048
- up_codes: bfloat16 [8192, 28672], P('dp', 'tensor'), may hold values from -8 to 7, as said below
- up_scales: float32 [64, 28672], P('dp', 'tensor'), may hold values from 0.0012 to 0.0048
- down_codes: bfloat16 [28672, 8192], P('tensor', 'dp'), may hold values from -8 to 7, as said below
- down_scales: float32 [224, 8192], P('tensor', 'dp'), may hold values from 0.0006 to 0.0024
Outputs:
- layer_out: bfloat16 [768, 8192], P('tensor', 'dp')
Inputs may be any that keep to these rules, and one draw needn't show every extreme that they name: `gate_codes`: every code is an integer. `up_codes`: every code is an integer. `down_codes`: every code is an integer.
All inputs are finite; a program needn't handle non-finite values.
Results may differ from a plain program's by a relative error of at most 0.04.
Values may be sent and summed in bfloat16 or wider, within the bound.
No kernel may reach another device: no remote copies, remote signals or barrier semaphores. Data moves between devices by JAX's collectives and lax.ppermute only.
A program may use at most 64 MiB of HBM per device.

v0:
```python
import math

import jax
import jax.numpy as jnp
import numpy as np
from jax import lax
from jax.sharding import PartitionSpec as P

HK = 28
HB = 1024
G = 128


def from_partner(value, axis, stride):
    return lax.ppermute(value, axis, [(i, i ^ 1 << stride) for i in range(lax.axis_size(axis))])


def paley_matrix():
    modulus = 13
    residues = set((number * number % modulus for number in range(1, modulus)))
    character = np.array([0] + [1 if number in residues else -1 for number in range(1, modulus)])
    jacobsthal = character[(np.arange(modulus)[:, None] - np.arange(modulus)[None, :]) % modulus]
    top_row = np.concatenate([np.zeros((1, 1)), np.ones((1, modulus))], axis=1)
    lower_rows = np.concatenate([np.ones((modulus, 1)), jacobsthal], axis=1)
    conference = np.concatenate([top_row, lower_rows], axis=0)
    first_part = np.kron(conference, np.array([[1.0, -1.0], [-1.0, -1.0]]))
    second_part = np.kron(np.eye(modulus + 1), np.array([[1.0, 1.0], [1.0, -1.0]]))
    return jnp.asarray(first_part + second_part, dtype=jnp.float32)


def walsh(extent):
    indices = jnp.arange(extent, dtype=jnp.int32)
    common = jnp.bitwise_and(indices[:, None], indices[None, :])
    parity = jnp.zeros((extent, extent), jnp.int32)
    for bit_pos in range(max(extent.bit_length() - 1, 0)):
        parity = parity + jnp.bitwise_and(jnp.right_shift(common, bit_pos), 1)
    return (1 - 2 * jnp.bitwise_and(parity, 1)).astype(jnp.float32)


def dequantize(codes, scales, group):
    row_count, col_count = codes.shape
    grouped = (
        codes.astype(jnp.float32).reshape(row_count // group, group, col_count) * scales[:, None, :]
    )
    return grouped.reshape(row_count, col_count).astype(jnp.bfloat16)


def per_device(drafts, gate_codes, gate_scales, up_codes, up_scales, down_codes, down_scales):
    tensor_n = lax.axis_size("tensor")
    unit_width = gate_codes.shape[1]
    both_weights = jnp.concatenate(
        [dequantize(gate_codes, gate_scales, G), dequantize(up_codes, up_scales, G)], axis=1
    )
    gathered = lax.all_gather(drafts, "tensor", axis=0, tiled=True)
    sums = lax.psum_scatter(
        jnp.dot(gathered, both_weights, preferred_element_type=jnp.float32).astype(jnp.bfloat16),
        "dp",
        scatter_dimension=0,
        tiled=True,
    ).astype(jnp.float32)
    gate = sums[:, :unit_width]
    up = sums[:, unit_width:]
    hidden = (jax.nn.silu(gate) * up).astype(jnp.bfloat16)
    row_count = hidden.shape[0]
    local_span = HB // tensor_n
    mixed = hidden.astype(jnp.float32).reshape(row_count, local_span, HK)
    mixed = jnp.einsum("rlk,ik->rli", mixed, paley_matrix(), precision=lax.Precision.HIGHEST)
    mixed = jnp.einsum("ml,rli->rmi", walsh(local_span), mixed, precision=lax.Precision.HIGHEST)
    scale_inv = 1.0 / math.sqrt(HK * HB)
    position = lax.axis_index("tensor")
    for bit_pos in range(tensor_n.bit_length() - 1):
        partner = from_partner(mixed.astype(jnp.bfloat16), "tensor", bit_pos).astype(mixed.dtype)
        upper = jnp.bitwise_and(jnp.right_shift(position, bit_pos), 1) == 1
        mixed = jnp.where(upper, partner - mixed, mixed + partner)
    rotated = (mixed * scale_inv).astype(jnp.bfloat16).reshape(row_count, unit_width)
    down_weights = dequantize(down_codes, down_scales, G)
    partial_value = jnp.dot(
        lax.all_gather(rotated, "dp", axis=0, tiled=True),
        down_weights,
        preferred_element_type=jnp.float32,
    )
    return lax.psum_scatter(
        partial_value.astype(jnp.bfloat16), "tensor", scatter_dimension=0, tiled=True
    )


def solution(mesh):
    return jax.shard_map(
        per_device,
        mesh=mesh,
        in_specs=(
            P("tensor", "dp"),
            P("dp", "tensor"),
            P("dp", "tensor"),
            P("dp", "tensor"),
            P("dp", "tensor"),
            P("tensor", "dp"),
            P("tensor", "dp"),
        ),
        out_specs=P("tensor", "dp"),
        check_vma=False,
    )
```

profile of v0, /device:TPU:2, one launch (start us, length us, event | category | flops | bytes accessed | tf_op | source)
XLA Modules:
  0.0 493.0 jit_solution(2328212934556906990)
XLA Ops:
  6.5 0.0 reduce-scatter.7.cloned.1.call-start
  6.5 92.4 %all_gather.6 = bf16[768,512]{1,0:T(8,128)(2,1)S(1)} all-gather(bf16[24,512]{1,0:T(8,128)(2,1)} %param.8), channel_id=1, replica_groups=mesh['dp'=16,'tensor'=32] {'tensor'}, dimensions={0}, use_global_device_ids=true | all-gather | bytes 811008 | tf_op jit(solution)/shard_map/all_gather | solution.py:54
  99.0 1.8 fusion.5
  100.8 1.7 fusion
  102.5 2.8 copy.17
  105.3 0.0 copy-start.2
  105.3 0.0 reduce-scatter.7.cloned.1.call-update
  105.3 0.0 all-gather.2.cloned.1.call-start
  105.4 92.5 %reduce-scatter.7.cloned.1.call-done = bf16[48,1792]{1,0:T(8,128)(2,1)} async-done(((bf16[768,1792]{1,0:T(8,128)(2,1)}), bf16[48,1792]{1,0:T(8,128)(2,1)}) %reduce-scatter.7.cloned.1.call-update) | async-done | bytes 172048 | tf_op jit(solution)/shard_map/reduce_scatter | solution.py:55
  197.8 0.9 convert_element_type.76
  198.8 0.1 fusion.16
  198.8 1.0 reshape.18
  199.8 0.0 copy-done.2
  199.8 0.5 fusion.54
  200.3 0.7 copy.15
  201.0 0.5 fusion.53
  201.5 3.1 collective-permute-start
  204.7 5.0 %collective-permute-done = bf16[48,32,28]{0,1,2:T(8,128)(2,1)S(1)} collective-permute-done((bf16[48,32,28]{0,1,2:T(8,128)(2,1)S(1)}, bf16[48,32,28]{0,1,2:T(8,128)(2,1)S(1)}, u32[]{:S(2)}, u32[]{:S(2)}) %collective-permute-start) | collective-permute-done | bytes 86048 | tf_op jit(solution)/shard_map/ppermute | solution.py:15
  209.6 0.1 fusion.17
  209.7 2.6 collective-permute-start.1
  212.3 10.4 %collective-permute-done.1 = bf16[48,32,28]{0,1,2:T(8,128)(2,1)S(1)} collective-permute-done((bf16[48,32,28]{0,1,2:T(8,128)(2,1)S(1)}, bf16[48,32,28]{0,1,2:T(8,128)(2,1)S(1)}, u32[]{:S(2)}, u32[]{:S(2)}) %collective-permute-start.1) | collective-permute-done | bytes 86048 | tf_op jit(solution)/shard_map/ppermute | solution.py:15
  222.7 0.1 fusion.15
  222.8 3.5 collective-permute-start.2
  226.3 5.2 %collective-permute-done.2 = bf16[48,32,28]{0,1,2:T(8,128)(2,1)S(1)} collective-permute-done((bf16[48,32,28]{0,1,2:T(8,128)(2,1)S(1)}, bf16[48,32,28]{0,1,2:T(8,128)(2,1)S(1)}, u32[]{:S(2)}, u32[]{:S(2)}) %collective-permute-start.2) | collective-permute-done | bytes 86048 | tf_op jit(solution)/shard_map/ppermute | solution.py:15
  231.6 0.2 fusion.51
  231.8 0.0 copy-start
  231.8 0.0 copy-start.1
  231.8 4.6 collective-permute-start.3
  236.4 9.1 %collective-permute-done.3 = bf16[48,32,28]{0,1,2:T(8,128)(2,1)S(1)} collective-permute-done((bf16[48,32,28]{0,1,2:T(8,128)(2,1)S(1)}, bf16[48,32,28]{0,1,2:T(8,128)(2,1)S(1)}, u32[]{:S(2)}, u32[]{:S(2)}) %collective-permute-start.3) | collective-permute-done | bytes 86048 | tf_op jit(solution)/shard_map/ppermute | solution.py:15
  245.5 0.1 fusion.14
  245.6 8.0 %collective-permute-start.4 = (bf16[48,32,28]{0,1,2:T(8,128)(2,1)S(1)}, bf16[48,32,28]{0,1,2:T(8,128)(2,1)S(1)}, u32[]{:S(2)}, u32[]{:S(2)}) collective-permute-start(bf16[48,32,28]{0,1,2:T(8,128)(2,1)S(1)} %fusion.14), channel_id=1, source_target_pairs={{0,16},{1,17},{2,18},{3,19},{4,20},{5,21},{6,22},{7,23},{8,24},{9,... | collective-permute-start | bytes 258056 | tf_op jit(solution)/shard_map/ppermute | solution.py:15
  253.6 10.6 %collective-permute-done.4 = bf16[48,32,28]{0,1,2:T(8,128)(2,1)S(1)} collective-permute-done((bf16[48,32,28]{0,1,2:T(8,128)(2,1)S(1)}, bf16[48,32,28]{0,1,2:T(8,128)(2,1)S(1)}, u32[]{:S(2)}, u32[]{:S(2)}) %collective-permute-start.4) | collective-permute-done | bytes 86048 | tf_op jit(solution)/shard_map/ppermute | solution.py:15
  264.2 0.2 fusion.13
  264.3 0.7 copy.16
  265.1 1.2 reshape.19
  266.3 0.0 all-gather.2.cloned.1.call-update
  266.3 0.0 reduce-scatter.5.cloned.1.call-start
  266.4 0.0 copy-done
  266.4 0.0 copy-done.1
  266.4 0.2 fusion.4
  266.6 57.6 %all-gather.2.cloned.1.call-done = bf16[768,896]{1,0:T(8,128)(2,1)} async-done(((bf16[48,896]{1,0:T(8,128)(2,1)}), bf16[768,896]{1,0:T(8,128)(2,1)}) %all-gather.2.cloned.1.call-update) | async-done | bytes 1376272 | tf_op jit(solution)/shard_map/all_gather | solution.py:78
  324.2 3.2 convolution_convert_fusion.1
  327.4 0.0 reduce-scatter.5.cloned.1.call-update
  327.4 159.0 %reduce-scatter.5.cloned.1.call-done = bf16[24,512]{1,0:T(8,128)(2,1)} async-done(((bf16[768,512]{1,0:T(8,128)(2,1)}), bf16[24,512]{1,0:T(8,128)(2,1)}) %reduce-scatter.5.cloned.1.call-update) | async-done | bytes 24592 | tf_op jit(solution)/shard_map/reduce_scatter | solution.py:82
Async XLA Ops:
  6.5 191.3 %reduce-scatter.7.cloned.1.call-start = ((), (), s32[]{:S(2)}) async-start(), calls=%async_computation.4 | async-start | bytes 2924544 | tf_op jit(solution)/shard_map/reduce_scatter | solution.py:55
  105.3 94.6 %copy-start.2 = (f32[28,28,1]{1,0,2:T(8,128)S(1)}, f32[28,28,1]{1,0,2:T(8,128)}, u32[]{:S(2)}) copy-start(f32[28,28,1]{1,0,2:T(8,128)} %constant.31) | copy-start | bytes 9412
  105.3 218.9 %all-gather.2.cloned.1.call-start = ((), (), s32[]{:S(2)}) async-start(), calls=%async_computation.2 | async-start | bytes 1462272 | tf_op jit(solution)/shard_map/all_gather | solution.py:78
  201.5 8.1 %collective-permute-start = (bf16[48,32,28]{0,1,2:T(8,128)(2,1)S(1)}, bf16[48,32,28]{0,1,2:T(8,128)(2,1)S(1)}, u32[]{:S(2)}, u32[]{:S(2)}) collective-permute-start(bf16[48,32,28]{0,1,2:T(8,128)(2,1)S(1)} %get-tuple-element.7), channel_id=1, source_target_pairs={{0,1},{1,0},{2,3},{3,2},{4,5},{5,4},{6,7},{7,6},{8,9},{9,8},{10,11... | collective-permute-start | bytes 258056 | tf_op jit(solution)/shard_map/ppermute | solution.py:15
  209.7 13.0 %collective-permute-start.1 = (bf16[48,32,28]{0,1,2:T(8,128)(2,1)S(1)}, bf16[48,32,28]{0,1,2:T(8,128)(2,1)S(1)}, u32[]{:S(2)}, u32[]{:S(2)}) collective-permute-start(bf16[48,32,28]{0,1,2:T(8,128)(2,1)S(1)} %fusion.17), channel_id=1, source_target_pairs={{0,2},{1,3},{2,0},{3,1},{4,6},{5,7},{6,4},{7,5},{8,10},{9,11},{10,... | collective-permute-start | bytes 258056 | tf_op jit(solution)/shard_map/ppermute | solution.py:15
  222.8 8.7 %collective-permute-start.2 = (bf16[48,32,28]{0,1,2:T(8,128)(2,1)S(1)}, bf16[48,32,28]{0,1,2:T(8,128)(2,1)S(1)}, u32[]{:S(2)}, u32[]{:S(2)}) collective-permute-start(bf16[48,32,28]{0,1,2:T(8,128)(2,1)S(1)} %fusion.15), channel_id=1, source_target_pairs={{0,4},{1,5},{2,6},{3,7},{4,0},{5,1},{6,2},{7,3},{8,12},{9,13},{10,... | collective-permute-start | bytes 258056 | tf_op jit(solution)/shard_map/ppermute | solution.py:15
  231.8 34.6 %copy-start = (bf16[896,512]{1,0:T(8,128)(2,1)S(1)}, bf16[896,512]{1,0:T(8,128)(2,1)}, u32[]{:S(2)}) copy-start(bf16[896,512]{1,0:T(8,128)(2,1)} %param.13) | copy-start | bytes 2752516
  231.8 34.6 %copy-start.1 = (f32[7,512]{1,0:T(8,128)S(1)}, f32[7,512]{1,0:T(8,128)}, u32[]{:S(2)}) copy-start(f32[7,512]{1,0:T(8,128)} %param.14) | copy-start | bytes 43012
  231.8 13.7 %collective-permute-start.3 = (bf16[48,32,28]{0,1,2:T(8,128)(2,1)S(1)}, bf16[48,32,28]{0,1,2:T(8,128)(2,1)S(1)}, u32[]{:S(2)}, u32[]{:S(2)}) collective-permute-start(bf16[48,32,28]{0,1,2:T(8,128)(2,1)S(1)} %get-tuple-element.5), channel_id=1, source_target_pairs={{0,8},{1,9},{2,10},{3,11},{4,12},{5,13},{6,14},{7,15},{8,0},{9,1},... | collective-permute-start | bytes 258056 | tf_op jit(solution)/shard_map/ppermute | solution.py:15
  245.6 18.6 %collective-permute-start.4 = (bf16[48,32,28]{0,1,2:T(8,128)(2,1)S(1)}, bf16[48,32,28]{0,1,2:T(8,128)(2,1)S(1)}, u32[]{:S(2)}, u32[]{:S(2)}) collective-permute-start(bf16[48,32,28]{0,1,2:T(8,128)(2,1)S(1)} %fusion.14), channel_id=1, source_target_pairs={{0,16},{1,17},{2,18},{3,19},{4,20},{5,21},{6,22},{7,23},{8,24},{9,... | collective-permute-start | bytes 258056 | tf_op jit(solution)/shard_map/ppermute | solution.py:15
  266.3 220.2 %reduce-scatter.5.cloned.1.call-start = ((), (), s32[]{:S(2)}) async-start(), calls=%async_computation.3 | async-start | bytes 811008 | tf_op jit(solution)/shard_map/reduce_scatter | solution.py:82
Sparse Core Ops, SparseCore 0:
  105.4 92.3 reduce-scatter.6
  266.4 57.7 all-gather.1
  327.5 158.8 reduce-scatter.4
where the time goes:
time: 493 us
  waiting for transfers between devices  349 us (71%)
  blocking collectives  92.4 us (19%)
  starting transfers between devices  21.8 us (4%)
  between operations  13.3 us (3%)
  local copies, waits for them, and re-layouts  6.45 us (1%)
  matrix products  5.85 us (1%)
    reduce_scatter x1, waiting for transfers between devices, per_device(): lax.psum_scatter(partial_value.astype(jnp.bfloat16), 'tensor', scatter_di...  159 us
    reduce_scatter x1, waiting for transfers between devices, per_device(): lax.psum_scatter(jnp.dot(gathered, both_weights, preferred_element_type=j...  92.5 us
    all_gather x1, blocking collectives, per_device(): gathered = lax.all_gather(drafts, 'tensor', axis=0, tiled=True)  92.4 us
    all_gather x1, waiting for transfers between devices, per_device(): lax.all_gather(rotated, 'dp', axis=0, tiled=True)  57.6 us
    ppermute x5, waiting for transfers between devices, from_partner(): lax.ppermute(value, axis, [(i, i ^ 1 << stride) for i in range(lax.axis_s...  40.3 us
    ppermute x5, starting transfers between devices, from_partner(): lax.ppermute(value, axis, [(i, i ^ 1 << stride) for i in range(lax.axis_s...  21.7 us
  transfers between devices with their start and end apart: 8, of which 8 were waited for; matrix products, arithmetic and copies ran while one was open for 0% of the time, Pallas kernels for 0%

commit v1 on v0

v1 whole, which is shorter than its diff:
```python
import math

import jax
import jax.numpy as jnp
import ml_dtypes
import numpy as np
from jax import lax
from jax.experimental import pallas as pl
from jax.experimental.pallas import tpu as pltpu
from jax.sharding import Mesh
from jax.sharding import PartitionSpec as P

HK = 28
HB = 1024
G = 128
N_T = 32
SPAN = HB // N_T
UNITS = SPAN * HK
GROUP = 56
GROUPS = UNITS // GROUP
LANES = 128
CORES = [(0, 1), (1, 0)]
SCALE = 1.0 / math.sqrt(HK * HB)


def paley_matrix():
    modulus = 13
    residues = set((number * number % modulus for number in range(1, modulus)))
    character = np.array([0] + [1 if number in residues else -1 for number in range(1, modulus)])
    jacobsthal = character[(np.arange(modulus)[:, None] - np.arange(modulus)[None, :]) % modulus]
    top_row = np.concatenate([np.zeros((1, 1)), np.ones((1, modulus))], axis=1)
    lower_rows = np.concatenate([np.ones((modulus, 1)), jacobsthal], axis=1)
    conference = np.concatenate([top_row, lower_rows], axis=0)
    first_part = np.kron(conference, np.array([[1.0, -1.0], [-1.0, -1.0]]))
    second_part = np.kron(np.eye(modulus + 1), np.array([[1.0, 1.0], [1.0, -1.0]]))
    return first_part + second_part


def walsh(extent):
    matrix = np.ones((1, 1))
    while matrix.shape[0] < extent:
        matrix = np.kron(np.array([[1.0, 1.0], [1.0, -1.0]]), matrix)
    return matrix


def block_matrix():
    return np.kron(walsh(SPAN), paley_matrix()).T.astype(ml_dtypes.bfloat16)


def dequantize(codes, scales):
    row_count, col_count = codes.shape
    grouped = (
        codes.astype(jnp.float32).reshape(row_count // G, G, col_count) * scales[:, None, :]
    )
    return grouped.reshape(row_count, col_count).astype(jnp.bfloat16)


def whole(memory=pltpu.VMEM):
    return pl.BlockSpec(memory_space=memory)


def call(kernel, out_shape, operands, flops, name):
    return pl.pallas_call(
        kernel,
        out_shape=jax.ShapeDtypeStruct(out_shape, jnp.bfloat16),
        in_specs=[whole()] * len(operands),
        out_specs=whole(),
        name=name,
        compiler_params=pltpu.CompilerParams(vmem_limit_bytes=32 * 1024 * 1024),
        cost_estimate=pl.CostEstimate(flops=flops, bytes_accessed=2_000_000, transcendentals=0),
    )(*operands)


def sum_and_cut(parts_ref, out_ref):
    total = parts_ref[0].astype(jnp.float32)
    for part in range(1, parts_ref.shape[0]):
        total = total + parts_ref[part].astype(jnp.float32)
    for group in range(GROUPS):
        start = 2 * GROUP * group
        tile, offset = start // LANES, start % LANES
        piece = total[:, tile * LANES : (tile + 1) * LANES]
        if offset:
            piece = pltpu.roll(piece, LANES - offset, 1)
            if offset + 2 * GROUP > LANES:
                after = total[:, (tile + 1) * LANES : (tile + 2) * LANES]
                after = pltpu.roll(after, LANES - offset, 1)
                lane = lax.broadcasted_iota(jnp.int32, piece.shape, 1)
                piece = jnp.where(lane < LANES - offset, piece, after)
        piece = piece.astype(jnp.bfloat16)
        for rows in range(4):
            out_ref[rows * GROUPS + group] = piece[rows * 24 : rows * 24 + 24]


def gate_and_mix(sums_ref, out_ref):
    sums = sums_ref[0].astype(jnp.float32) + sums_ref[1].astype(jnp.float32)
    lane = lax.broadcasted_iota(jnp.int32, (N_T, 8, LANES), 2)
    packed = []
    for tile in range(3):
        gate = sums[:, tile * 8 : tile * 8 + 8]
        up = pltpu.roll(gate, LANES - GROUP, 2)
        value = (gate / (1.0 + jnp.exp(-gate)) * up).astype(jnp.bfloat16).astype(jnp.float32)
        value = jnp.where(lane < GROUP, value, 0.0)
        half = 1
        while half < N_T:
            split = value.reshape(N_T // (2 * half), 2, half, 8, LANES)
            low, high = split[:, 0], split[:, 1]
            value = jnp.stack([low + high, low - high], axis=1).reshape(N_T, 8, LANES)
            half *= 2
        packed.append(value * SCALE)
    first = jnp.where(lane < GROUP, packed[0], pltpu.roll(packed[1], GROUP, 2))
    both = jnp.concatenate([first, packed[2]], axis=1).astype(jnp.bfloat16)
    out_ref[0] = both
    out_ref[1] = both


def join_and_mix(pieces_ref, matrix_ref, out_ref):
    lane = lax.broadcasted_iota(jnp.int32, (8, LANES), 1)
    rows = []
    for block in range(4):
        tiles = [[None] * (UNITS // LANES) for _ in range(3)]
        for group in range(GROUPS):
            piece = pieces_ref[block * GROUPS + group].astype(jnp.float32)
            start = GROUP * group
            tile, offset = start // LANES, start % LANES
            for row, (source, shift) in enumerate(((0, 0), (0, GROUP), (1, 0))):
                moved = piece[source * 8 : source * 8 + 8]
                turn = (offset - shift) % LANES
                if turn:
                    moved = pltpu.roll(moved, turn, 1)
                line = tiles[row]
                line[tile] = moved if line[tile] is None else jnp.where(lane < offset, line[tile], moved)
                if offset + GROUP > LANES:
                    line[tile + 1] = moved
        rows += [jnp.concatenate(line, axis=1) for line in tiles]
    units = jnp.concatenate(rows, axis=0).astype(jnp.bfloat16)
    mixed = jnp.dot(units, matrix_ref[...], preferred_element_type=jnp.float32).astype(jnp.bfloat16)
    for copy in range(out_ref.shape[0]):
        out_ref[copy] = mixed


def per_device(drafts, gate_codes, gate_scales, up_codes, up_scales, down_codes, down_scales):
    core = lax.axis_index("c")
    depth = drafts.shape[1]
    rows = drafts.shape[0] * N_T
    half = rows // 2
    gathered = lax.all_to_all(
        jnp.broadcast_to(drafts[None], (N_T,) + drafts.shape), ("z", "yl"), 0, 0, tiled=True
    ).reshape(rows, depth)
    both_weights = jnp.concatenate(
        [
            dequantize(gate_codes, gate_scales).reshape(depth, GROUPS, GROUP),
            dequantize(up_codes, up_scales).reshape(depth, GROUPS, GROUP),
        ],
        axis=2,
    ).reshape(depth, 2 * UNITS)
    theirs = lax.dynamic_slice_in_dim(gathered, (1 - core) * half, half, 0)
    ours = lax.dynamic_slice_in_dim(gathered, core * half, half, 0)
    sent = jnp.dot(theirs, both_weights, preferred_element_type=jnp.float32).astype(jnp.bfloat16)
    received = lax.ppermute(sent, "c", CORES)
    kept = jnp.dot(ours, both_weights, preferred_element_type=jnp.float32)
    sums = (kept + received.astype(jnp.float32)).astype(jnp.bfloat16)
    sums = lax.all_to_all(sums.reshape(4, half // 4, 2 * UNITS), "x", 0, 0, tiled=True)
    pieces = call(sum_and_cut, (4 * GROUPS, 24, LANES), (sums,), 1_000_000, "sum_and_cut")
    pieces = lax.all_to_all(pieces, ("yh", "z", "yl"), 0, 0, tiled=True)
    pieces = call(
        gate_and_mix, (2, N_T, 16, LANES), (pieces.reshape(2, N_T, 24, LANES),), 2_000_000, "gate_and_mix"
    )
    pieces = lax.all_to_all(pieces.reshape(2 * N_T, 16, LANES), ("yh", "z", "yl"), 0, 0, tiled=True)
    rotated = call(
        join_and_mix,
        (4, half // 4, UNITS),
        (pieces, jnp.asarray(block_matrix())),
        200_000_000,
        "join_and_mix",
    )
    rotated = lax.all_to_all(rotated, "x", 0, 0, tiled=True).reshape(half, UNITS)
    other = lax.ppermute(rotated, "c", CORES)
    down_weights = dequantize(down_codes, down_scales)
    own_part = jnp.dot(rotated, down_weights, preferred_element_type=jnp.float32)
    other_part = jnp.dot(other, down_weights, preferred_element_type=jnp.float32)
    own_part, other_part = own_part.astype(jnp.bfloat16), other_part.astype(jnp.bfloat16)
    partial_value = jnp.zeros((rows, own_part.shape[1]), jnp.bfloat16)
    partial_value = lax.dynamic_update_slice_in_dim(partial_value, own_part, core * half, 0)
    partial_value = lax.dynamic_update_slice_in_dim(partial_value, other_part, (1 - core) * half, 0)
    partial_value = lax.all_to_all(
        partial_value.reshape(N_T, rows // N_T, own_part.shape[1]), ("z", "yl"), 0, 0, tiled=True
    )
    return jnp.sum(partial_value.astype(jnp.float32), axis=0).astype(jnp.bfloat16)


def solution(mesh):
    fine = Mesh(mesh.devices.reshape(2, 4, 2, 8, 4), ("yh", "x", "c", "z", "yl"))
    dp, tensor = ("yh", "x", "c"), ("z", "yl")
    return jax.shard_map(
        per_device,
        mesh=fine,
        in_specs=(
            P(tensor, dp),
            P(dp, tensor),
            P(dp, tensor),
            P(dp, tensor),
            P(dp, tensor),
            P(tensor, dp),
            P(tensor, dp),
        ),
        out_specs=P(tensor, dp),
        check_vma=False,
    )
```

time: 493 us -> 159 us (0.32)
  the two profiles are of different devices: /device:TPU:2 before, /device:TPU:16 now
where the time goes in v1:
time: 159 us; the launch traced here: 158 us
  blocking collectives  105 us (66%)
  waiting for transfers between devices  20.5 us (13%)
  starting transfers between devices  17.8 us (11%)
  local copies, waits for them, and re-layouts  6.43 us (4%)
  matrix products  5.4 us (3%)
  other arithmetic  1.79 us (1%)
    all_to_all x1, blocking collectives, per_device(): lax.all_to_all(partial_value.reshape(N_T, rows // N_T, own_part.shape[1])...  27.8 us
    all_to_all x1, blocking collectives, per_device(): pieces = lax.all_to_all(pieces, ('yh', 'z', 'yl'), 0, 0, tiled=True)  24.1 us
    all_to_all x1, blocking collectives, per_device(): lax.all_to_all(sums.reshape(4, half // 4, 2 * UNITS), 'x', 0, 0, tiled=True)  23 us
    all_to_all x1, blocking collectives, per_device(): lax.all_to_all(pieces.reshape(2 * N_T, 16, LANES), ('yh', 'z', 'yl'), 0,...  18.4 us
    all_to_all x1, waiting for transfers between devices, per_device(): lax.all_to_all(jnp.broadcast_to(drafts[None], (N_T,) + drafts.shape), ('z...  15.8 us
    all_to_all x1, starting transfers between devices, per_device(): lax.all_to_all(jnp.broadcast_to(drafts[None], (N_T,) + drafts.shape), ('z...  14 us
    all_to_all x1, blocking collectives, per_device(): lax.all_to_all(rotated, 'x', 0, 0, tiled=True).reshape(half, UNITS)  11.5 us
    ppermute x1, waiting for transfers between devices, per_device(): received = lax.ppermute(sent, 'c', CORES)  3.43 us
  transfers between devices with their start and end apart: 3, of which 3 were waited for; matrix products, arithmetic and copies ran while one was open for 4% of the time, Pallas kernels for 0%

profile of v1, /device:TPU:16, one launch (start us, length us, event | category | flops | bytes accessed | tf_op | source)
XLA Modules:
  0.0 158.0 jit_solution(1014886905675512499)
XLA Ops:
  0.0 0.0 copy-start.4
  0.0 0.0 copy-start.1
  0.0 1.7 %broadcast_in_dim.5 = bf16[32,24,512]{2,1,0:T(8,128)(2,1)} broadcast(bf16[24,512]{1,0:T(8,128)(2,1)} %param.8), dimensions={1,2} | broadcast | bytes 811008 | tf_op jit(solution)/shard_map/broadcast_in_dim | solution.py:147
  1.8 0.0 copy-start.5
  1.8 14.0 %all-to-all-start = ((bf16[32,24,512]{2,1,0:T(8,128)(2,1)}), bf16[32,24,512]{2,1,0:T(8,128)(2,1)S(1)}, u32[]{:S(2)}, u32[]{:S(2)}) async-start(bf16[32,24,512]{2,1,0:T(8,128)(2,1)} %broadcast_in_dim.5), calls=%async_computation | async-start | bytes 1572864 | tf_op jit(solution)/shard_map/all_to_all | solution.py:146
  15.7 0.0 copy-done.4
  15.8 0.2 copy.10
  16.0 0.0 copy-done.1
  16.0 0.5 copy.9
  16.5 0.0 copy-done.5
  16.5 0.2 copy.12
  16.7 1.5 copy.11
  18.2 1.1 mul.42
  19.3 0.4 fusion.1
  19.7 1.1 mul.45
  20.8 0.4 fusion
  21.2 0.2 pad_maximum_fusion
  21.3 15.8 %all-to-all-done = bf16[32,24,512]{2,1,0:T(8,128)(2,1)S(1)} async-done(((bf16[32,24,512]{2,1,0:T(8,128)(2,1)}), bf16[32,24,512]{2,1,0:T(8,128)(2,1)S(1)}, u32[]{:S(2)}, u32[]{:S(2)}) %all-to-all-start) | async-done | bytes 786464 | tf_op jit(solution)/shard_map/all_to_all | solution.py:146
  37.1 2.0 %convolution_convert_fusion = bf16[384,1792]{1,0:T(8,128)(2,1)} fusion(bf16[512,1792]{0,1:T(8,128)(2,1)S(1)} %bitcast.40, bf16[768,512]{1,0:T(8,128)(2,1)S(1)} %bitcast.43, s32[]{:T(128)S(6)} %select_n.9), kind=kOutput, calls=%fused_computation | convolution fusion | flops 705331200 | bytes 3604484 | tf_op jit(solution)/shard_map/dot_general | solution.py:158
  39.2 1.9 %collective-permute-start = (bf16[384,1792]{1,0:T(8,128)(2,1)}, bf16[384,1792]{1,0:T(8,128)(2,1)}, u32[]{:S(2)}, u32[]{:S(2)}) collective-permute-start(bf16[384,1792]{1,0:T(8,128)(2,1)} %convolution_convert_fusion), channel_id=1, source_target_pairs={{0,32},{32,0},{1,33},{33,1},{2,34},{34,2},{3,35},{35,3},{4,36},{36... | collective-permute-start | bytes 4128776 | tf_op jit(solution)/shard_map/ppermute | solution.py:159
  41.1 3.4 %collective-permute-done = bf16[384,1792]{1,0:T(8,128)(2,1)} collective-permute-done((bf16[384,1792]{1,0:T(8,128)(2,1)}, bf16[384,1792]{1,0:T(8,128)(2,1)}, u32[]{:S(2)}, u32[]{:S(2)}) %collective-permute-start) | collective-permute-done | bytes 1376288 | tf_op jit(solution)/shard_map/ppermute | solution.py:159
  44.5 2.2 %add_convert_fusion = bf16[384,1792]{1,0:T(8,128)(2,1)S(1)} fusion(bf16[384,1792]{1,0:T(8,128)(2,1)} %collective-permute-done, bf16[512,1792]{0,1:T(8,128)(2,1)S(1)} %bitcast.41, bf16[768,512]{1,0:T(8,128)(2,1)S(1)} %bitcast.44, s32[]{:T(128)S(6)} %select_n.8), kind=kOutput, calls=%fused_computation.1 | convolution fusion | flops 706707456 | bytes 4980740 | tf_op jit(solution)/shard_map/dot_general | solution.py:160
  46.8 23.0 %all_to_all.30.parts_ref = bf16[4,96,1792]{2,1,0:T(8,128)(2,1)S(1)} all-to-all(bf16[4,96,1792]{2,1,0:T(8,128)(2,1)S(1)} %bitcast.42), channel_id=1, replica_groups=mesh['yh'=2,'x'=4,'c'=2,'z'=8,'yl'=4] {'x'}, dimensions={0} | all-to-all | bytes 2752512 | tf_op jit(solution)/shard_map/all_to_all | solution.py:162
  69.8 0.0 copy-start
  69.8 0.3 sum_and_cut.1
  70.1 24.1 %all_to_all.31 = bf16[64,24,128]{2,1,0:T(8,128)(2,1)S(1)} all-to-all(bf16[64,24,128]{2,1,0:T(8,128)(2,1)S(1)} %sum_and_cut.1), channel_id=1, replica_groups=mesh['yh'=2,'x'=4,'c'=2,'z'=8,'yl'=4] {'yh','z','yl'}, dimensions={0} | all-to-all | bytes 786432 | tf_op jit(solution)/shard_map/all_to_all | solution.py:164
  94.1 0.3 gate_and_mix.1
  94.4 18.4 %all_to_all.32.pieces_ref = bf16[64,16,128]{2,1,0:T(8,128)(2,1)S(1)} all-to-all(bf16[64,16,128]{2,1,0:T(8,128)(2,1)S(1)} %bitcast.34), channel_id=1, replica_groups=mesh['yh'=2,'x'=4,'c'=2,'z'=8,'yl'=4] {'yh','z','yl'}, dimensions={0} | all-to-all | bytes 524288 | tf_op jit(solution)/shard_map/all_to_all | solution.py:168
  112.9 0.0 copy-done
  112.9 0.0 copy-start.2
  112.9 0.0 copy-start.3
  112.9 0.5 join_and_mix.1
  113.3 11.5 %all_to_all.33 = bf16[4,96,896]{2,1,0:T(8,128)(2,1)S(1)} all-to-all(bf16[4,96,896]{2,1,0:T(8,128)(2,1)S(1)} %join_and_mix.1), channel_id=1, replica_groups=mesh['yh'=2,'x'=4,'c'=2,'z'=8,'yl'=4] {'x'}, dimensions={0} | all-to-all | bytes 1376256 | tf_op jit(solution)/shard_map/all_to_all | solution.py:176
  124.9 1.9 %collective-permute-start.1 = (bf16[384,896]{1,0:T(8,128)(2,1)S(1)}, bf16[384,896]{1,0:T(8,128)(2,1)S(1)}, u32[]{:S(2)}, u32[]{:S(2)}) collective-permute-start(bf16[384,896]{1,0:T(8,128)(2,1)S(1)} %bitcast.45), channel_id=1, source_target_pairs={{0,32},{32,0},{1,33},{33,1},{2,34},{34,2},{3,35},{35,3},{4,36},{36... | collective-permute-start | bytes 2064392 | tf_op jit(solution)/shard_map/ppermute | solution.py:177
  126.8 0.0 copy-done.2
  126.8 0.0 copy-done.3
  126.8 0.2 fusion.2
  127.0 0.1 broadcast_in_dim.4
  127.1 0.6 fusion.4
  127.6 1.3 collective-permute-done.1
  128.9 0.6 fusion.3
  129.5 27.8 %all_to_all.34 = bf16[32,24,512]{2,1,0:T(8,128)(2,1)S(1)} all-to-all(bf16[32,24,512]{2,1,0:T(8,128)(2,1)S(1)} %bitcast.39), channel_id=1, replica_groups=mesh['yh'=2,'x'=4,'c'=2,'z'=8,'yl'=4] {'z','yl'}, dimensions={0} | all-to-all | bytes 1572864 | tf_op jit(solution)/shard_map/all_to_all | solution.py:185
  157.3 0.7 reduce_sum.12
Async XLA Ops:
  0.0 15.7 %copy-start.4 = (f32[4,896]{1,0:T(4,128)S(1)}, f32[4,896]{1,0:T(4,128)}, u32[]{:S(2)}) copy-start(f32[4,896]{1,0:T(4,128)} %param.10) | copy-start | bytes 43012
  0.0 16.0 %copy-start.1 = (bf16[512,896]{1,0:T(8,128)(2,1)S(1)}, bf16[512,896]{1,0:T(8,128)(2,1)}, u32[]{:S(2)}) copy-start(bf16[512,896]{1,0:T(8,128)(2,1)} %param.9) | copy-start | bytes 2752516
  1.8 14.8 %copy-start.5 = (f32[4,896]{1,0:T(4,128)S(1)}, f32[4,896]{1,0:T(4,128)}, u32[]{:S(2)}) copy-start(f32[4,896]{1,0:T(4,128)} %param.12) | copy-start | bytes 43012
  1.8 35.4 %all-to-all-start = ((bf16[32,24,512]{2,1,0:T(8,128)(2,1)}), bf16[32,24,512]{2,1,0:T(8,128)(2,1)S(1)}, u32[]{:S(2)}, u32[]{:S(2)}) async-start(bf16[32,24,512]{2,1,0:T(8,128)(2,1)} %broadcast_in_dim.5), calls=%async_computation | async-start | bytes 1572864 | tf_op jit(solution)/shard_map/all_to_all | solution.py:146
  39.2 5.4 %collective-permute-start = (bf16[384,1792]{1,0:T(8,128)(2,1)}, bf16[384,1792]{1,0:T(8,128)(2,1)}, u32[]{:S(2)}, u32[]{:S(2)}) collective-permute-start(bf16[384,1792]{1,0:T(8,128)(2,1)} %convolution_convert_fusion), channel_id=1, source_target_pairs={{0,32},{32,0},{1,33},{33,1},{2,34},{34,2},{3,35},{35,3},{4,36},{36... | collective-permute-start | bytes 4128776 | tf_op jit(solution)/shard_map/ppermute | solution.py:159
  69.8 43.1 %copy-start = (bf16[896,896]{1,0:T(8,128)(2,1)S(1)}, bf16[896,896]{1,0:T(8,128)(2,1)}, u32[]{:S(2)}) copy-start(bf16[896,896]{1,0:T(8,128)(2,1)} %constant.20.clone.matrix_ref) | copy-start | bytes 4816900
  112.9 13.9 %copy-start.2 = (bf16[896,512]{1,0:T(8,128)(2,1)S(1)}, bf16[896,512]{1,0:T(8,128)(2,1)}, u32[]{:S(2)}) copy-start(bf16[896,512]{1,0:T(8,128)(2,1)} %param.13) | copy-start | bytes 2752516
  112.9 13.9 %copy-start.3 = (f32[7,512]{1,0:T(8,128)S(1)}, f32[7,512]{1,0:T(8,128)}, u32[]{:S(2)}) copy-start(f32[7,512]{1,0:T(8,128)} %param.14) | copy-start | bytes 43012
  124.9 4.0 %collective-permute-start.1 = (bf16[384,896]{1,0:T(8,128)(2,1)S(1)}, bf16[384,896]{1,0:T(8,128)(2,1)S(1)}, u32[]{:S(2)}, u32[]{:S(2)}) collective-permute-start(bf16[384,896]{1,0:T(8,128)(2,1)S(1)} %bitcast.45), channel_id=1, source_target_pairs={{0,32},{32,0},{1,33},{33,1},{2,34},{34,2},{3,35},{35,3},{4,36},{36... | collective-permute-start | bytes 2064392 | tf_op jit(solution)/shard_map/ppermute | solution.py:177

commit v2 on v1

--- a/solution.py
+++ b/solution.py
@@ -1,3 +1,4 @@
+import functools
 import math
 
 import jax
@@ -59,16 +60,51 @@
     return pl.BlockSpec(memory_space=memory)
 
 
-def call(kernel, out_shape, operands, flops, name):
+def call(kernel, name, out_shape, operands, flops, dtype=jnp.bfloat16, memory=pltpu.VMEM, scratch=()):
     return pl.pallas_call(
         kernel,
-        out_shape=jax.ShapeDtypeStruct(out_shape, jnp.bfloat16),
+        out_shape=jax.ShapeDtypeStruct(out_shape, dtype),
         in_specs=[whole()] * len(operands),
-        out_specs=whole(),
+        out_specs=whole(memory),
+        scratch_shapes=list(scratch),
         name=name,
         compiler_params=pltpu.CompilerParams(vmem_limit_bytes=32 * 1024 * 1024),
         cost_estimate=pl.CostEstimate(flops=flops, bytes_accessed=2_000_000, transcendentals=0),
     )(*operands)
+
+
+def copy_out(block_ref, out_ref, held, sems):
+    at_once = held.shape[0]
+    for index in range(at_once):
+        held[index] = block_ref[...]
+    copies = [
+        pltpu.make_async_copy(held, out_ref.at[pl.ds(at_once * index, at_once)], sems.at[index])
+        for index in range(out_ref.shape[0] // at_once)
+    ]
+    for copy in copies:
+        copy.start()
+    for copy in copies:
+        copy.wait()
+
+
+def rows_times(flip, rows_ref, weights_ref, out_ref):
+    half = out_ref.shape[0]
+    core = lax.axis_index("c")
+    mine = 1 - core if flip else core
+    rows = rows_ref[pl.ds(pl.multiple_of(mine * half, half), half), :]
+    out_ref[...] = jnp.dot(rows, weights_ref[...], preferred_element_type=jnp.float32).astype(out_ref.dtype)
+
+
+def add_parts(kept_ref, received_ref, out_ref, held, sems):
+    blocks, size = out_ref.shape[0], out_ref.shape[1]
+    copies = []
+    for block in range(blocks):
+        rows = pl.ds(block * size, size)
+        held[block] = (kept_ref[rows, :] + received_ref[rows, :].astype(jnp.float32)).astype(jnp.bfloat16)
+        copies.append(pltpu.make_async_copy(held.at[block], out_ref.at[block], sems.at[block]))
+        copies[-1].start()
+    for copy in copies:
+        copy.wait()
 
 
 def sum_and_cut(parts_ref, out_ref):
@@ -92,7 +128,7 @@
 
 
 def gate_and_mix(sums_ref, out_ref):
-    sums = sums_ref[0].astype(jnp.float32) + sums_ref[1].astype(jnp.float32)
+    sums = sums_ref[:, 0].astype(jnp.float32) + sums_ref[:, 1].astype(jnp.float32)
     lane = lax.broadcasted_iota(jnp.int32, (N_T, 8, LANES), 2)
     packed = []
     for tile in range(3):
@@ -109,8 +145,8 @@
         packed.append(value * SCALE)
     first = jnp.where(lane < GROUP, packed[0], pltpu.roll(packed[1], GROUP, 2))
     both = jnp.concatenate([first, packed[2]], axis=1).astype(jnp.bfloat16)
-    out_ref[0] = both
-    out_ref[1] = both
+    out_ref[:, 0] = both
+    out_ref[:, 1] = both
 
 
 def join_and_mix(pieces_ref, matrix_ref, out_ref):
@@ -143,9 +179,17 @@
     depth = drafts.shape[1]
     rows = drafts.shape[0] * N_T
     half = rows // 2
-    gathered = lax.all_to_all(
-        jnp.broadcast_to(drafts[None], (N_T,) + drafts.shape), ("z", "yl"), 0, 0, tiled=True
-    ).reshape(rows, depth)
+    everyone = ("z", "yl", "yh")
+    copies = call(
+        copy_out,
+        "copy_out",
+        (N_T,) + drafts.shape,
+        (drafts,),
+        1_000,
+        memory=pltpu.HBM,
+        scratch=[pltpu.VMEM((8,) + drafts.shape, drafts.dtype), pltpu.SemaphoreType.DMA((N_T // 8,))],
+    )
+    gathered = lax.all_to_all(copies, ("z", "yl"), 0, 0, tiled=True).reshape(rows, depth)
     both_weights = jnp.concatenate(
         [
             dequantize(gate_codes, gate_scales).reshape(depth, GROUPS, GROUP),
@@ -153,25 +197,37 @@
         ],
         axis=2,
     ).reshape(depth, 2 * UNITS)
-    theirs = lax.dynamic_slice_in_dim(gathered, (1 - core) * half, half, 0)
-    ours = lax.dynamic_slice_in_dim(gathered, core * half, half, 0)
-    sent = jnp.dot(theirs, both_weights, preferred_element_type=jnp.float32).astype(jnp.bfloat16)
+    flops = rows * depth * 2 * UNITS
+    sent = call(
+        functools.partial(rows_times, True), "their_rows", (half, 2 * UNITS), (gathered, both_weights), flops
+    )
     received = lax.ppermute(sent, "c", CORES)
-    kept = jnp.dot(ours, both_weights, preferred_element_type=jnp.float32)
-    sums = (kept + received.astype(jnp.float32)).astype(jnp.bfloat16)
-    sums = lax.all_to_all(sums.reshape(4, half // 4, 2 * UNITS), "x", 0, 0, tiled=True)
-    pieces = call(sum_and_cut, (4 * GROUPS, 24, LANES), (sums,), 1_000_000, "sum_and_cut")
-    pieces = lax.all_to_all(pieces, ("yh", "z", "yl"), 0, 0, tiled=True)
+    kept = call(
+        functools.partial(rows_times, False),
+        "our_rows",
+        (half, 2 * UNITS),
+        (gathered, both_weights),
+        flops,
+        dtype=jnp.float32,
+    )
+    sums = call(
+        add_parts,
+        "add_parts",
+        (4, half // 4, 2 * UNITS),
+        (kept, received),
+        1_000_000,
+        memory=pltpu.HBM,
+        scratch=[pltpu.VMEM((4, half // 4, 2 * UNITS), jnp.bfloat16), pltpu.SemaphoreType.DMA((4,))],
+    )
+    sums = lax.all_to_all(sums, "x", 0, 0, tiled=True)
+    pieces = call(sum_and_cut, "sum_and_cut", (4 * GROUPS, 24, LANES), (sums,), 1_000_000)
+    pieces = lax.all_to_all(pieces, everyone, 0, 0, tiled=True)
     pieces = call(
-        gate_and_mix, (2, N_T, 16, LANES), (pieces.reshape(2, N_T, 24, LANES),), 2_000_000, "gate_and_mix"
-    )
-    pieces = lax.all_to_all(pieces.reshape(2 * N_T, 16, LANES), ("yh", "z", "yl"), 0, 0, tiled=True)
+        gate_and_mix, "gate_and_mix", (N_T, 2, 16, LANES), (pieces.reshape(N_T, 2, 24, LANES),), 2_000_000
+    )
+    pieces = lax.all_to_all(pieces.reshape(2 * N_T, 16, LANES), everyone, 0, 0, tiled=True)
     rotated = call(
-        join_and_mix,
-        (4, half // 4, UNITS),
-        (pieces, jnp.asarray(block_matrix())),
-        200_000_000,
-        "join_and_mix",
+        join_and_mix, "join_and_mix", (4, half // 4, UNITS), (pieces, jnp.asarray(block_matrix())), 200_000_000
     )
     rotated = lax.all_to_all(rotated, "x", 0, 0, tiled=True).reshape(half, UNITS)
     other = lax.ppermute(rotated, "c", CORES)

time: 159 us -> 155 us (0.975)
  waiting for transfers between devices: 20.5 us -> 15.3 us
  matrix products: 5.4 us -> 1.13 us
  Pallas kernels: 1.02 us -> 4.49 us
  local copies, waits for them, and re-layouts: 6.43 us -> 8.19 us
    dot_general x2 -> x0, matrix products: 4.27 us -> none  [the longest x1 2.25 us: per_device(): kept = jnp.dot(ours, both_weights, preferred_element_type=jnp.float32)]
    all_to_all x1, waiting for transfers between devices: 15.8 us -> 11.8 us  [per_device(): lax.all_to_all(copies, ('z', 'yl'), 0, 0, tiled=True).reshape(rows, depth)]
    pallas_call x3 -> x7, Pallas kernels: 1.02 us -> 4.49 us  [call(): pl.pallas_call(kernel, out_shape=jax.ShapeDtypeStruct(out_shape, dtype),...]
    reshape x0 -> x1, local copies, waits for them, and re-layouts: none -> 2.77 us  [per_device(): both_weights = jnp.concatenate([dequantize(gate_codes, gate_scales).resha...]
    broadcast_in_dim x1 -> x0, local copies, waits for them, and re-layouts: 1.75 us -> none  [per_device(): jnp.broadcast_to(drafts[None], (N_T,) + drafts.shape)]
  transfers between devices with their start and end apart: 3 -> 3, of which waited for: 3 -> 3; matrix products, arithmetic and copies ran while one was open for 4% -> 7% of each run, Pallas kernels for 0% -> 1%
where the time goes in v2:
time: 155 us
  blocking collectives  105 us (68%)
  starting transfers between devices  17.7 us (11%)
  waiting for transfers between devices  15.3 us (10%)
  local copies, waits for them, and re-layouts  8.19 us (5%)
  Pallas kernels  4.49 us (3%)
  other arithmetic  3.03 us (2%)
    all_to_all x1, blocking collectives, per_device(): lax.all_to_all(partial_value.reshape(N_T, rows // N_T, own_part.shape[1])...  28.3 us
    all_to_all x1, blocking collectives, per_device(): pieces = lax.all_to_all(pieces, everyone, 0, 0, tiled=True)  23.6 us
    all_to_all x1, blocking collectives, per_device(): sums = lax.all_to_all(sums, 'x', 0, 0, tiled=True)  23 us
    all_to_all x1, blocking collectives, per_device(): lax.all_to_all(pieces.reshape(2 * N_T, 16, LANES), everyone, 0, 0, tiled=...  18.3 us
    all_to_all x1, starting transfers between devices, per_device(): lax.all_to_all(copies, ('z', 'yl'), 0, 0, tiled=True).reshape(rows, depth)  13.9 us
    all_to_all x1, waiting for transfers between devices, per_device(): lax.all_to_all(copies, ('z', 'yl'), 0, 0, tiled=True).reshape(rows, depth)  11.8 us
    all_to_all x1, blocking collectives, per_device(): lax.all_to_all(rotated, 'x', 0, 0, tiled=True).reshape(half, UNITS)  11.3 us
    pallas_call x7, Pallas kernels, call(): pl.pallas_call(kernel, out_shape=jax.ShapeDtypeStruct(out_shape, dtype),...  4.49 us
  transfers between devices with their start and end apart: 3, of which 3 were waited for; matrix products, arithmetic and copies ran while one was open for 7% of the time, Pallas kernels for 1%

profile of v2, /device:TPU:16, one launch (start us, length us, event | category | flops | bytes accessed | tf_op | source)
XLA Modules:
  0.0 154.5 jit_solution(12033786686239471598)
XLA Ops:
  0.0 0.0 copy-start.1
  0.0 0.7 copy-done.1
  0.7 0.0 copy-start.5
  0.7 0.0 copy-start.2
  0.7 0.9 copy_out.1
  1.7 0.0 copy-start.6
  1.7 13.9 %all-to-all-start = ((bf16[32,24,512]{2,1,0:T(8,128)(2,1)}), bf16[32,24,512]{2,1,0:T(8,128)(2,1)S(1)}, u32[]{:S(2)}, u32[]{:S(2)}) async-start(bf16[32,24,512]{2,1,0:T(8,128)(2,1)} %copy_out.1), calls=%async_computation | async-start | bytes 1572864 | tf_op jit(solution)/shard_map/all_to_all | solution.py:192
  15.6 0.0 copy-done.5
  15.6 0.2 copy.10
  15.8 0.0 copy-done.2
  15.8 0.5 copy.9
  16.3 0.0 copy-done.6
  16.3 0.2 copy.12
  16.6 1.5 copy.11
  18.0 1.1 mul.39
  19.1 0.4 fusion.1
  19.5 1.1 mul.42
  20.6 0.4 fusion
  21.0 1.4 pad_maximum_fusion
  22.4 2.8 %copy.13.weights_ref = bf16[512,1792]{1,0:T(8,128)(2,1)S(1)} copy(bf16[512,1792]{0,1:T(8,128)(2,1)} %bitcast.34) | data formatting | bytes 3670016 | tf_op jit(solution)/shard_map/reshape | solution.py:199
  25.2 11.8 %all-to-all-done = bf16[32,24,512]{2,1,0:T(8,128)(2,1)S(1)} async-done(((bf16[32,24,512]{2,1,0:T(8,128)(2,1)}), bf16[32,24,512]{2,1,0:T(8,128)(2,1)S(1)}, u32[]{:S(2)}, u32[]{:S(2)}) %all-to-all-start) | async-done | bytes 786464 | tf_op jit(solution)/shard_map/all_to_all | solution.py:192
  37.0 0.9 their_rows.1
  37.9 1.9 %collective-permute-start = (bf16[384,1792]{1,0:T(8,128)(2,1)S(1)}, bf16[384,1792]{1,0:T(8,128)(2,1)S(1)}, u32[]{:S(2)}, u32[]{:S(2)}) collective-permute-start(bf16[384,1792]{1,0:T(8,128)(2,1)S(1)} %their_rows.1), channel_id=1, source_target_pairs={{0,32},{32,0},{1,33},{33,1},{2,34},{34,2},{3,35},{35,3},{4,36},{36... | collective-permute-start | bytes 4128776 | tf_op jit(solution)/shard_map/ppermute | solution.py:204
  39.8 0.9 our_rows.1.kept_ref
  40.7 2.2 %collective-permute-done.received_ref = bf16[384,1792]{1,0:T(8,128)(2,1)S(1)} collective-permute-done((bf16[384,1792]{1,0:T(8,128)(2,1)S(1)}, bf16[384,1792]{1,0:T(8,128)(2,1)S(1)}, u32[]{:S(2)}, u32[]{:S(2)}) %collective-permute-start) | collective-permute-done | bytes 1376288 | tf_op jit(solution)/shard_map/ppermute | solution.py:204
  42.9 0.8 add_parts.1
  43.7 23.0 %all_to_all.30.parts_ref = bf16[4,96,1792]{2,1,0:T(8,128)(2,1)S(1)} all-to-all(bf16[4,96,1792]{2,1,0:T(8,128)(2,1)S(1)} %add_parts.1), channel_id=1, replica_groups=mesh['yh'=2,'x'=4,'c'=2,'z'=8,'yl'=4] {'x'}, dimensions={0} | all-to-all | bytes 2752512 | tf_op jit(solution)/shard_map/all_to_all | solution.py:222
  66.7 0.0 copy-start
  66.7 0.3 sum_and_cut.1
  67.0 23.6 %all_to_all.31 = bf16[64,24,128]{2,1,0:T(8,128)(2,1)S(1)} all-to-all(bf16[64,24,128]{2,1,0:T(8,128)(2,1)S(1)} %sum_and_cut.1), channel_id=1, replica_groups=mesh['yh'=2,'x'=4,'c'=2,'z'=8,'yl'=4] {'z','yl','yh'}, dimensions={0} | all-to-all | bytes 786432 | tf_op jit(solution)/shard_map/all_to_all | solution.py:224
  90.6 0.3 gate_and_mix.1
  90.8 18.3 %all_to_all.32.pieces_ref = bf16[64,16,128]{2,1,0:T(8,128)(2,1)S(1)} all-to-all(bf16[64,16,128]{2,1,0:T(8,128)(2,1)S(1)} %bitcast.33), channel_id=1, replica_groups=mesh['yh'=2,'x'=4,'c'=2,'z'=8,'yl'=4] {'z','yl','yh'}, dimensions={0} | all-to-all | bytes 524288 | tf_op jit(solution)/shard_map/all_to_all | solution.py:228
  109.1 0.0 copy-done
  109.1 0.0 copy-start.3
  109.1 0.0 copy-start.4
  109.1 0.5 join_and_mix.1
  109.6 11.3 %all_to_all.33 = bf16[4,96,896]{2,1,0:T(8,128)(2,1)S(1)} all-to-all(bf16[4,96,896]{2,1,0:T(8,128)(2,1)S(1)} %join_and_mix.1), channel_id=1, replica_groups=mesh['yh'=2,'x'=4,'c'=2,'z'=8,'yl'=4] {'x'}, dimensions={0} | all-to-all | bytes 1376256 | tf_op jit(solution)/shard_map/all_to_all | solution.py:232
  120.9 1.9 %collective-permute-start.1 = (bf16[384,896]{1,0:T(8,128)(2,1)S(1)}, bf16[384,896]{1,0:T(8,128)(2,1)S(1)}, u32[]{:S(2)}, u32[]{:S(2)}) collective-permute-start(bf16[384,896]{1,0:T(8,128)(2,1)S(1)} %bitcast.40), channel_id=1, source_target_pairs={{0,32},{32,0},{1,33},{33,1},{2,34},{34,2},{3,35},{35,3},{4,36},{36... | collective-permute-start | bytes 2064392 | tf_op jit(solution)/shard_map/ppermute | solution.py:233
  122.8 0.0 copy-done.3
  122.9 0.0 copy-done.4
  122.9 0.2 fusion.2
  123.0 0.1 broadcast_in_dim.2
  123.1 0.6 fusion.4
  123.7 1.3 collective-permute-done.1
  124.9 0.6 fusion.3
  125.5 28.3 %all_to_all.34 = bf16[32,24,512]{2,1,0:T(8,128)(2,1)S(1)} all-to-all(bf16[32,24,512]{2,1,0:T(8,128)(2,1)S(1)} %bitcast.39), channel_id=1, replica_groups=mesh['yh'=2,'x'=4,'c'=2,'z'=8,'yl'=4] {'z','yl'}, dimensions={0} | all-to-all | bytes 1572864 | tf_op jit(solution)/shard_map/all_to_all | solution.py:241
  153.8 0.7 reduce_sum.12
Async XLA Ops:
  0.0 0.7 copy-start.1
  0.7 14.8 %copy-start.5 = (f32[4,896]{1,0:T(4,128)S(1)}, f32[4,896]{1,0:T(4,128)}, u32[]{:S(2)}) copy-start(f32[4,896]{1,0:T(4,128)} %param.10) | copy-start | bytes 43012
  0.7 15.1 %copy-start.2 = (bf16[512,896]{1,0:T(8,128)(2,1)S(1)}, bf16[512,896]{1,0:T(8,128)(2,1)}, u32[]{:S(2)}) copy-start(bf16[512,896]{1,0:T(8,128)(2,1)} %param.9) | copy-start | bytes 2752516
  1.7 14.7 %copy-start.6 = (f32[4,896]{1,0:T(4,128)S(1)}, f32[4,896]{1,0:T(4,128)}, u32[]{:S(2)}) copy-start(f32[4,896]{1,0:T(4,128)} %param.12) | copy-start | bytes 43012
  1.7 35.3 %all-to-all-start = ((bf16[32,24,512]{2,1,0:T(8,128)(2,1)}), bf16[32,24,512]{2,1,0:T(8,128)(2,1)S(1)}, u32[]{:S(2)}, u32[]{:S(2)}) async-start(bf16[32,24,512]{2,1,0:T(8,128)(2,1)} %copy_out.1), calls=%async_computation | async-start | bytes 1572864 | tf_op jit(solution)/shard_map/all_to_all | solution.py:192
  37.9 5.0 %collective-permute-start = (bf16[384,1792]{1,0:T(8,128)(2,1)S(1)}, bf16[384,1792]{1,0:T(8,128)(2,1)S(1)}, u32[]{:S(2)}, u32[]{:S(2)}) collective-permute-start(bf16[384,1792]{1,0:T(8,128)(2,1)S(1)} %their_rows.1), channel_id=1, source_target_pairs={{0,32},{32,0},{1,33},{33,1},{2,34},{34,2},{3,35},{35,3},{4,36},{36... | collective-permute-start | bytes 4128776 | tf_op jit(solution)/shard_map/ppermute | solution.py:204
  66.7 42.5 %copy-start = (bf16[896,896]{1,0:T(8,128)(2,1)S(1)}, bf16[896,896]{1,0:T(8,128)(2,1)}, u32[]{:S(2)}) copy-start(bf16[896,896]{1,0:T(8,128)(2,1)} %constant.20.clone.matrix_ref) | copy-start | bytes 4816900
  109.1 13.7 %copy-start.3 = (bf16[896,512]{1,0:T(8,128)(2,1)S(1)}, bf16[896,512]{1,0:T(8,128)(2,1)}, u32[]{:S(2)}) copy-start(bf16[896,512]{1,0:T(8,128)(2,1)} %param.13) | copy-start | bytes 2752516
  109.1 13.7 %copy-start.4 = (f32[7,512]{1,0:T(8,128)S(1)}, f32[7,512]{1,0:T(8,128)}, u32[]{:S(2)}) copy-start(f32[7,512]{1,0:T(8,128)} %param.14) | copy-start | bytes 43012
  120.9 4.0 %collective-permute-start.1 = (bf16[384,896]{1,0:T(8,128)(2,1)S(1)}, bf16[384,896]{1,0:T(8,128)(2,1)S(1)}, u32[]{:S(2)}, u32[]{:S(2)}) collective-permute-start(bf16[384,896]{1,0:T(8,128)(2,1)S(1)} %bitcast.40), channel_id=1, source_target_pairs={{0,32},{32,0},{1,33},{33,1},{2,34},{34,2},{3,35},{35,3},{4,36},{36... | collective-permute-start | bytes 2064392 | tf_op jit(solution)/shard_map/ppermute | solution.py:233

commit v3 on v2

--- a/solution.py
+++ b/solution.py
@@ -60,12 +60,18 @@
     return pl.BlockSpec(memory_space=memory)
 
 
-def call(kernel, name, out_shape, operands, flops, dtype=jnp.bfloat16, memory=pltpu.VMEM, scratch=()):
+def call(kernel, name, out_shape, operands, flops, memory=pltpu.VMEM, scratch=(), specs=None):
+    places = specs or [pltpu.VMEM] * len(operands)
+    if isinstance(out_shape, list):
+        shapes = [jax.ShapeDtypeStruct(shape, dtype) for shape, dtype in out_shape]
+        results = [whole(memory)] * len(shapes)
+    else:
+        shapes, results = jax.ShapeDtypeStruct(out_shape, jnp.bfloat16), whole(memory)
     return pl.pallas_call(
         kernel,
-        out_shape=jax.ShapeDtypeStruct(out_shape, dtype),
-        in_specs=[whole()] * len(operands),
-        out_specs=whole(memory),
+        out_shape=shapes,
+        in_specs=[whole(place) for place in places],
+        out_specs=results,
         scratch_shapes=list(scratch),
         name=name,
         compiler_params=pltpu.CompilerParams(vmem_limit_bytes=32 * 1024 * 1024),
@@ -87,42 +93,58 @@
         copy.wait()
 
 
-def rows_times(flip, rows_ref, weights_ref, out_ref):
+def dequantize_pair(gate_ref, gate_scales_ref, up_ref, up_scales_ref, out_ref):
+    for group in range(gate_scales_ref.shape[0]):
+        rows = pl.ds(group * G, G)
+        line = slice(group, group + 1)
+        gate = gate_ref[rows, :].astype(jnp.float32) * gate_scales_ref[line, :]
+        up = up_ref[rows, :].astype(jnp.float32) * up_scales_ref[line, :]
+        out_ref[rows, :UNITS] = gate.astype(jnp.bfloat16)
+        out_ref[rows, UNITS:] = up.astype(jnp.bfloat16)
+
+
+def take_theirs(rows_ref, out_ref):
     half = out_ref.shape[0]
-    core = lax.axis_index("c")
-    mine = 1 - core if flip else core
-    rows = rows_ref[pl.ds(pl.multiple_of(mine * half, half), half), :]
-    out_ref[...] = jnp.dot(rows, weights_ref[...], preferred_element_type=jnp.float32).astype(out_ref.dtype)
-
-
-def add_parts(kept_ref, received_ref, out_ref, held, sems):
-    blocks, size = out_ref.shape[0], out_ref.shape[1]
+    start = (1 - lax.axis_index("c")) * half
+    out_ref[...] = rows_ref[pl.ds(pl.multiple_of(start, half), half), :]
+
+
+def times_own(after_ref, rows_ref, weights_ref, other_ref, out_ref, held_ref, sems):
+    step = other_ref.shape[0] // sems.shape[0]
     copies = []
-    for block in range(blocks):
-        rows = pl.ds(block * size, size)
-        held[block] = (kept_ref[rows, :] + received_ref[rows, :].astype(jnp.float32)).astype(jnp.bfloat16)
-        copies.append(pltpu.make_async_copy(held.at[block], out_ref.at[block], sems.at[block]))
+    for index in range(sems.shape[0]):
+        lines = pl.ds(index * step, step)
+        copies.append(pltpu.make_async_copy(other_ref.at[lines], held_ref.at[lines], sems.at[index]))
         copies[-1].start()
+    half = out_ref.shape[0]
+    start = lax.axis_index("c") * half
+    rows = rows_ref[pl.ds(pl.multiple_of(start, half), half), :]
+    out_ref[...] = jnp.dot(rows, weights_ref[...], preferred_element_type=jnp.float32)
     for copy in copies:
         copy.wait()
+
+
+def add_other(part_ref, rows_ref, weights_ref, out_ref):
+    total = part_ref[...] + jnp.dot(rows_ref[...], weights_ref[...], preferred_element_type=jnp.float32)
+    out_ref[...] = total.astype(jnp.bfloat16)
 
 
 def sum_and_cut(parts_ref, out_ref):
     total = parts_ref[0].astype(jnp.float32)
     for part in range(1, parts_ref.shape[0]):
         total = total + parts_ref[part].astype(jnp.float32)
+    lane = lax.broadcasted_iota(jnp.int32, (total.shape[0], LANES), 1)
     for group in range(GROUPS):
-        start = 2 * GROUP * group
-        tile, offset = start // LANES, start % LANES
-        piece = total[:, tile * LANES : (tile + 1) * LANES]
-        if offset:
-            piece = pltpu.roll(piece, LANES - offset, 1)
-            if offset + 2 * GROUP > LANES:
-                after = total[:, (tile + 1) * LANES : (tile + 2) * LANES]
-                after = pltpu.roll(after, LANES - offset, 1)
-                lane = lax.broadcasted_iota(jnp.int32, piece.shape, 1)
-                piece = jnp.where(lane < LANES - offset, piece, after)
-        piece = piece.astype(jnp.bfloat16)
+        offset = GROUP * group % LANES
+        halves = []
+        for base, shift in ((0, 0), (UNITS, GROUP)):
+            tile = (base + GROUP * group) // LANES * LANES
+            piece = total[:, tile : tile + LANES]
+            if offset + GROUP > LANES:
+                piece = jnp.where(lane < offset, total[:, tile + LANES : tile + 2 * LANES], piece)
+            turn = (shift - offset) % LANES
+            halves.append(pltpu.roll(piece, turn, 1) if turn else piece)
+        piece = jnp.where(lane < GROUP, halves[0], halves[1]).astype(jnp.bfloat16)
         for rows in range(4):
             out_ref[rows * GROUPS + group] = piece[rows * 24 : rows * 24 + 24]
 
@@ -179,6 +201,7 @@
     depth = drafts.shape[1]
     rows = drafts.shape[0] * N_T
     half = rows // 2
+    width = 2 * UNITS
     everyone = ("z", "yl", "yh")
     copies = call(
         copy_out,
@@ -190,36 +213,28 @@
         scratch=[pltpu.VMEM((8,) + drafts.shape, drafts.dtype), pltpu.SemaphoreType.DMA((N_T // 8,))],
     )
     gathered = lax.all_to_all(copies, ("z", "yl"), 0, 0, tiled=True).reshape(rows, depth)
-    both_weights = jnp.concatenate(
-        [
-            dequantize(gate_codes, gate_scales).reshape(depth, GROUPS, GROUP),
-            dequantize(up_codes, up_scales).reshape(depth, GROUPS, GROUP),
-        ],
-        axis=2,
-    ).reshape(depth, 2 * UNITS)
-    flops = rows * depth * 2 * UNITS
-    sent = call(
-        functools.partial(rows_times, True), "their_rows", (half, 2 * UNITS), (gathered, both_weights), flops
-    )
-    received = lax.ppermute(sent, "c", CORES)
-    kept = call(
-        functools.partial(rows_times, False),
-        "our_rows",
-        (half, 2 * UNITS),
-        (gathered, both_weights),
+    weights = call(
+        dequantize_pair,
+        "dequantize_pair",
+        (depth, width),
+        (gate_codes, gate_scales, up_codes, up_scales),
+        3_000_000,
+    )
+    other_weights = lax.ppermute(weights, "c", CORES)
+    flops = 2 * half * depth * width
+    theirs = call(take_theirs, "take_theirs", (half, depth), (gathered,), 1_000)
+    other_rows = lax.ppermute(theirs, "c", CORES)
+    part, other_weights = call(
+        times_own,
+        "times_own",
+        [((half, width), jnp.float32), ((depth, width), jnp.bfloat16)],
+        (theirs, gathered, weights, other_weights),
         flops,
-        dtype=jnp.float32,
-    )
-    sums = call(
-        add_parts,
-        "add_parts",
-        (4, half // 4, 2 * UNITS),
-        (kept, received),
-        1_000_000,
-        memory=pltpu.HBM,
-        scratch=[pltpu.VMEM((4, half // 4, 2 * UNITS), jnp.bfloat16), pltpu.SemaphoreType.DMA((4,))],
-    )
-    sums = lax.all_to_all(sums, "x", 0, 0, tiled=True)
+        specs=[pl.ANY, pltpu.VMEM, pltpu.VMEM, pltpu.HBM],
+        scratch=[pltpu.SemaphoreType.DMA((4,))],
+    )
+    sums = call(add_other, "add_other", (half, width), (part, other_rows, other_weights), flops)
+    sums = lax.all_to_all(sums.reshape(4, half // 4, width), "x", 0, 0, tiled=True)
     pieces = call(sum_and_cut, "sum_and_cut", (4 * GROUPS, 24, LANES), (sums,), 1_000_000)
     pieces = lax.all_to_all(pieces, everyone, 0, 0, tiled=True)
     pieces = call(

time: 155 us -> 154 us (level)
  local copies, waits for them, and re-layouts: 8.19 us -> 2.78 us
  waiting for transfers between devices: 15.3 us -> 18.5 us
  other arithmetic: 3.03 us -> 0.9 us
  starting transfers between devices: 17.7 us -> 19.6 us
    all_to_all x1, waiting for transfers between devices: 11.8 us -> 17.2 us  [per_device(): lax.all_to_all(copies, ('z', 'yl'), 0, 0, tiled=True).reshape(rows, depth)]
    reshape x1 -> x0, local copies, waits for them, and re-layouts: 2.77 us -> none  [per_device(): both_weights = jnp.concatenate([dequantize(gate_codes, gate_scales).resha...]
    ppermute x1 -> x2, waiting for transfers between devices: 2.21 us -> 0.01 us  [the longest x1 0.01 us: per_device(): other_weights = lax.ppermute(weights, 'c', CORES)]
    mul x2 -> x0, local copies, waits for them, and re-layouts: 2.2 us -> none  [dequantize(): codes.astype(jnp.float32).reshape(row_count // G, G, col_count)]
    ppermute x1 -> x2, starting transfers between devices: 1.92 us -> 3.84 us  [the longest x1 1.92 us: per_device(): other_weights = lax.ppermute(weights, 'c', CORES)]
    pallas_call x7 -> x8, Pallas kernels: 4.49 us -> 5.16 us  [call(): pl.pallas_call(kernel, out_shape=shapes, in_specs=[whole(place) for place...]
    unnamed x18 -> x16, local copies, waits for them, and re-layouts: 3.17 us -> 2.72 us
  transfers between devices with their start and end apart: 3 -> 4, of which waited for: 3 -> 2; matrix products, arithmetic and copies ran while one was open for 7% -> 1% of each run, Pallas kernels for 1% -> 1%
where the time goes in v3:
time: 154 us; the launch traced here: 153 us
  blocking collectives  105 us (68%)
  starting transfers between devices  19.6 us (13%)
  waiting for transfers between devices  18.5 us (12%)
  Pallas kernels  5.16 us (3%)
  local copies, waits for them, and re-layouts  2.78 us (2%)
    all_to_all x1, blocking collectives, per_device(): lax.all_to_all(partial_value.reshape(N_T, rows // N_T, own_part.shape[1])...  28.4 us
    all_to_all x1, blocking collectives, per_device(): pieces = lax.all_to_all(pieces, everyone, 0, 0, tiled=True)  23.7 us
    all_to_all x1, blocking collectives, per_device(): lax.all_to_all(sums.reshape(4, half // 4, width), 'x', 0, 0, tiled=True)  23.4 us
    all_to_all x1, blocking collectives, per_device(): lax.all_to_all(pieces.reshape(2 * N_T, 16, LANES), everyone, 0, 0, tiled=...  18.3 us
    all_to_all x1, waiting for transfers between devices, per_device(): lax.all_to_all(copies, ('z', 'yl'), 0, 0, tiled=True).reshape(rows, depth)  17.2 us
    all_to_all x1, starting transfers between devices, per_device(): lax.all_to_all(copies, ('z', 'yl'), 0, 0, tiled=True).reshape(rows, depth)  13.9 us
    all_to_all x1, blocking collectives, per_device(): lax.all_to_all(rotated, 'x', 0, 0, tiled=True).reshape(half, UNITS)  11.3 us
    pallas_call x8, Pallas kernels, call(): pl.pallas_call(kernel, out_shape=shapes, in_specs=[whole(place) for place...  5.16 us
  transfers between devices with their start and end apart: 4, of which 2 were waited for; matrix products, arithmetic and copies ran while one was open for 1% of the time, Pallas kernels for 1%

profile of v3, /device:TPU:16, one launch (start us, length us, event | category | flops | bytes accessed | tf_op | source)
XLA Modules:
  0.0 153.4 jit_solution(8526648067290015948)
XLA Ops:
  0.0 0.0 copy-start.1
  0.0 0.0 copy-start.3
  0.0 0.8 copy-done.3
  0.8 0.0 copy-start.4
  0.8 0.9 copy_out.1
  1.8 13.9 %all-to-all-start = ((bf16[32,24,512]{2,1,0:T(8,128)(2,1)}), bf16[32,24,512]{2,1,0:T(8,128)(2,1)S(1)}, u32[]{:S(2)}, u32[]{:S(2)}) async-start(bf16[32,24,512]{2,1,0:T(8,128)(2,1)} %copy_out.1), calls=%async_computation | async-start | bytes 1572864 | tf_op jit(solution)/shard_map/all_to_all | solution.py:215
  15.6 0.0 copy-done.1
  15.6 0.0 copy-done.4
  15.7 0.0 copy-start.2
  15.7 1.2 copy-done.2
  16.8 0.0 copy-start.5
  16.8 0.7 copy-done.5
  17.6 0.3 dequantize_pair.1.weights_ref
  17.9 1.9 %collective-permute-start = (bf16[512,1792]{1,0:T(8,128)(2,1)S(1)}, bf16[512,1792]{1,0:T(8,128)(2,1)}, u32[]{:S(2)}, u32[]{:S(2)}) collective-permute-start(bf16[512,1792]{1,0:T(8,128)(2,1)S(1)} %dequantize_pair.1.weights_ref), channel_id=1, source_target_pairs={{0,32},{32,0},{1,33},{33,1},{2,34},{34,2},{3,35},{35,3},{4,36},{36... | collective-permute-start | bytes 5505032 | tf_op jit(solution)/shard_map/ppermute | solution.py:223
  19.8 17.2 %all-to-all-done = bf16[32,24,512]{2,1,0:T(8,128)(2,1)S(1)} async-done(((bf16[32,24,512]{2,1,0:T(8,128)(2,1)}), bf16[32,24,512]{2,1,0:T(8,128)(2,1)S(1)}, u32[]{:S(2)}, u32[]{:S(2)}) %all-to-all-start) | async-done | bytes 786464 | tf_op jit(solution)/shard_map/all_to_all | solution.py:215
  37.1 1.9 %collective-permute-start.1 = (bf16[384,512]{1,0:T(8,128)(2,1)S(1)}, bf16[384,512]{1,0:T(8,128)(2,1)S(1)}, u32[]{:S(2)}, u32[]{:S(2)}) collective-permute-start(bf16[384,512]{1,0:T(8,128)(2,1)S(1)} %take_theirs.1.after_ref), channel_id=1, source_target_pairs={{0,32},{32,0},{1,33},{33,1},{2,34},{34,2},{3,35},{35,3},{4,36},{36... | collective-permute-start | bytes 1179656 | tf_op jit(solution)/shard_map/ppermute | solution.py:226
  39.0 0.0 collective-permute-done.other_ref
  39.0 1.9 %times_own.1 = (f32[384,1792]{1,0:T(8,128)S(1)}, bf16[512,1792]{1,0:T(8,128)(2,1)S(1)}) custom-call(bf16[384,512]{1,0:T(8,128)(2,1)S(1)} %take_theirs.1.after_ref, bf16[768,512]{1,0:T(8,128)(2,1)S(1)} %bitcast.15, bf16[512,1792]{1,0:T(8,128)(2,1)S(1)} %dequantize_pair.1.weights_ref, bf16[512,1792]{1,0:T(8,128)(2,1)} %collective-permute-done.other_ref), custom_call_target="tpu_custom_call" | custom-call | flops 704643072 | bytes 2000000 | tf_op jit(solution)/shard_map/times_own/pallas_call | solution.py:70
  40.9 0.0 collective-permute-done.1.rows_ref
  41.0 0.9 add_other.1
  41.8 23.4 %all_to_all.30.parts_ref = bf16[4,96,1792]{2,1,0:T(8,128)(2,1)S(1)} all-to-all(bf16[4,96,1792]{2,1,0:T(8,128)(2,1)S(1)} %bitcast.16), channel_id=1, replica_groups=mesh['yh'=2,'x'=4,'c'=2,'z'=8,'yl'=4] {'x'}, dimensions={0} | all-to-all | bytes 2752512 | tf_op jit(solution)/shard_map/all_to_all | solution.py:237
  65.2 0.0 copy-start
  65.2 0.4 sum_and_cut.1
  65.6 23.7 %all_to_all.31 = bf16[64,24,128]{2,1,0:T(8,128)(2,1)S(1)} all-to-all(bf16[64,24,128]{2,1,0:T(8,128)(2,1)S(1)} %sum_and_cut.1), channel_id=1, replica_groups=mesh['yh'=2,'x'=4,'c'=2,'z'=8,'yl'=4] {'z','yl','yh'}, dimensions={0} | all-to-all | bytes 786432 | tf_op jit(solution)/shard_map/all_to_all | solution.py:239
  89.3 0.3 gate_and_mix.1
  89.6 18.3 %all_to_all.32.pieces_ref = bf16[64,16,128]{2,1,0:T(8,128)(2,1)S(1)} all-to-all(bf16[64,16,128]{2,1,0:T(8,128)(2,1)S(1)} %bitcast.18), channel_id=1, replica_groups=mesh['yh'=2,'x'=4,'c'=2,'z'=8,'yl'=4] {'z','yl','yh'}, dimensions={0} | all-to-all | bytes 524288 | tf_op jit(solution)/shard_map/all_to_all | solution.py:243
  107.8 0.0 copy-done
  107.8 0.0 copy-start.6
  107.8 0.0 copy-start.7
  107.8 0.5 join_and_mix.1
  108.3 11.3 %all_to_all.33 = bf16[4,96,896]{2,1,0:T(8,128)(2,1)S(1)} all-to-all(bf16[4,96,896]{2,1,0:T(8,128)(2,1)S(1)} %join_and_mix.1), channel_id=1, replica_groups=mesh['yh'=2,'x'=4,'c'=2,'z'=8,'yl'=4] {'x'}, dimensions={0} | all-to-all | bytes 1376256 | tf_op jit(solution)/shard_map/all_to_all | solution.py:247
  119.6 1.9 %collective-permute-start.2 = (bf16[384,896]{1,0:T(8,128)(2,1)S(1)}, bf16[384,896]{1,0:T(8,128)(2,1)S(1)}, u32[]{:S(2)}, u32[]{:S(2)}) collective-permute-start(bf16[384,896]{1,0:T(8,128)(2,1)S(1)} %bitcast.20), channel_id=1, source_target_pairs={{0,32},{32,0},{1,33},{33,1},{2,34},{34,2},{3,35},{35,3},{4,36},{36... | collective-permute-start | bytes 2064392 | tf_op jit(solution)/shard_map/ppermute | solution.py:248
  121.5 0.0 copy-done.6
  121.5 0.0 copy-done.7
  121.6 0.2 fusion
  121.7 0.1 broadcast_in_dim.4
  121.8 0.6 fusion.2
  122.4 1.3 collective-permute-done.2
  123.6 0.6 fusion.1
  124.2 28.4 %all_to_all.34 = bf16[32,24,512]{2,1,0:T(8,128)(2,1)S(1)} all-to-all(bf16[32,24,512]{2,1,0:T(8,128)(2,1)S(1)} %bitcast.19), channel_id=1, replica_groups=mesh['yh'=2,'x'=4,'c'=2,'z'=8,'yl'=4] {'z','yl'}, dimensions={0} | all-to-all | bytes 1572864 | tf_op jit(solution)/shard_map/all_to_all | solution.py:256
  152.6 0.7 reduce_sum.12
  (1 shorter events, 0.0 us)
Async XLA Ops:
  0.0 15.6 %copy-start.1 = (bf16[512,896]{1,0:T(8,128)(2,1)S(1)}, bf16[512,896]{1,0:T(8,128)(2,1)}, u32[]{:S(2)}) copy-start(bf16[512,896]{1,0:T(8,128)(2,1)} %gate_ref.1) | copy-start | bytes 2752516
  0.0 0.8 copy-start.3
  0.8 14.8 %copy-start.4 = (f32[4,896]{1,0:T(4,128)S(1)}, f32[4,896]{1,0:T(4,128)}, u32[]{:S(2)}) copy-start(f32[4,896]{1,0:T(4,128)} %gate_scales_ref.1) | copy-start | bytes 43012
  1.8 35.3 %all-to-all-start = ((bf16[32,24,512]{2,1,0:T(8,128)(2,1)}), bf16[32,24,512]{2,1,0:T(8,128)(2,1)S(1)}, u32[]{:S(2)}, u32[]{:S(2)}) async-start(bf16[32,24,512]{2,1,0:T(8,128)(2,1)} %copy_out.1), calls=%async_computation | async-start | bytes 1572864 | tf_op jit(solution)/shard_map/all_to_all | solution.py:215
  15.7 1.2 copy-start.2
  16.8 0.7 copy-start.5
  17.9 21.1 %collective-permute-start = (bf16[512,1792]{1,0:T(8,128)(2,1)S(1)}, bf16[512,1792]{1,0:T(8,128)(2,1)}, u32[]{:S(2)}, u32[]{:S(2)}) collective-permute-start(bf16[512,1792]{1,0:T(8,128)(2,1)S(1)} %dequantize_pair.1.weights_ref), channel_id=1, source_target_pairs={{0,32},{32,0},{1,33},{33,1},{2,34},{34,2},{3,35},{35,3},{4,36},{36... | collective-permute-start | bytes 5505032 | tf_op jit(solution)/shard_map/ppermute | solution.py:223
  37.1 3.9 %collective-permute-start.1 = (bf16[384,512]{1,0:T(8,128)(2,1)S(1)}, bf16[384,512]{1,0:T(8,128)(2,1)S(1)}, u32[]{:S(2)}, u32[]{:S(2)}) collective-permute-start(bf16[384,512]{1,0:T(8,128)(2,1)S(1)} %take_theirs.1.after_ref), channel_id=1, source_target_pairs={{0,32},{32,0},{1,33},{33,1},{2,34},{34,2},{3,35},{35,3},{4,36},{36... | collective-permute-start | bytes 1179656 | tf_op jit(solution)/shard_map/ppermute | solution.py:226
  65.2 42.6 %copy-start = (bf16[896,896]{1,0:T(8,128)(2,1)S(1)}, bf16[896,896]{1,0:T(8,128)(2,1)}, u32[]{:S(2)}) copy-start(bf16[896,896]{1,0:T(8,128)(2,1)} %constant.20.clone.matrix_ref) | copy-start | bytes 4816900
  107.8 13.7 %copy-start.6 = (bf16[896,512]{1,0:T(8,128)(2,1)S(1)}, bf16[896,512]{1,0:T(8,128)(2,1)}, u32[]{:S(2)}) copy-start(bf16[896,512]{1,0:T(8,128)(2,1)} %param.13) | copy-start | bytes 2752516
  107.8 13.7 %copy-start.7 = (f32[7,512]{1,0:T(8,128)S(1)}, f32[7,512]{1,0:T(8,128)}, u32[]{:S(2)}) copy-start(f32[7,512]{1,0:T(8,128)} %param.14) | copy-start | bytes 43012
  119.6 4.0 %collective-permute-start.2 = (bf16[384,896]{1,0:T(8,128)(2,1)S(1)}, bf16[384,896]{1,0:T(8,128)(2,1)S(1)}, u32[]{:S(2)}, u32[]{:S(2)}) collective-permute-start(bf16[384,896]{1,0:T(8,128)(2,1)S(1)} %bitcast.20), channel_id=1, source_target_pairs={{0,32},{32,0},{1,33},{33,1},{2,34},{34,2},{3,35},{35,3},{4,36},{36... | collective-permute-start | bytes 2064392 | tf_op jit(solution)/shard_map/ppermute | solution.py:248

commit v4 on v3

--- a/solution.py
+++ b/solution.py
@@ -1,4 +1,3 @@
-import functools
 import math
 
 import jax
@@ -103,19 +102,31 @@
         out_ref[rows, UNITS:] = up.astype(jnp.bfloat16)
 
 
-def take_theirs(rows_ref, out_ref):
+def dequantize_one(codes_ref, scales_ref, out_ref):
+    for group in range(scales_ref.shape[0]):
+        rows = pl.ds(group * G, G)
+        weights = codes_ref[rows, :].astype(jnp.float32) * scales_ref[group : group + 1, :]
+        out_ref[rows, :] = weights.astype(jnp.bfloat16)
+
+
+def take_theirs(after_ref, rows_ref, out_ref):
     half = out_ref.shape[0]
     start = (1 - lax.axis_index("c")) * half
     out_ref[...] = rows_ref[pl.ds(pl.multiple_of(start, half), half), :]
 
 
-def times_own(after_ref, rows_ref, weights_ref, other_ref, out_ref, held_ref, sems):
-    step = other_ref.shape[0] // sems.shape[0]
+def fetch(source_ref, target_ref, sems):
+    step = source_ref.shape[0] // sems.shape[0]
     copies = []
     for index in range(sems.shape[0]):
         lines = pl.ds(index * step, step)
-        copies.append(pltpu.make_async_copy(other_ref.at[lines], held_ref.at[lines], sems.at[index]))
+        copies.append(pltpu.make_async_copy(source_ref.at[lines], target_ref.at[lines], sems.at[index]))
         copies[-1].start()
+    return copies
+
+
+def times_own(after_ref, rows_ref, weights_ref, other_ref, out_ref, held_ref, sems):
+    copies = fetch(other_ref, held_ref, sems)
     half = out_ref.shape[0]
     start = lax.axis_index("c") * half
     rows = rows_ref[pl.ds(pl.multiple_of(start, half), half), :]
@@ -127,6 +138,18 @@
 def add_other(part_ref, rows_ref, weights_ref, out_ref):
     total = part_ref[...] + jnp.dot(rows_ref[...], weights_ref[...], preferred_element_type=jnp.float32)
     out_ref[...] = total.astype(jnp.bfloat16)
+
+
+def times_down(after_ref, rows_ref, weights_ref, out_ref):
+    total = jnp.dot(rows_ref[...], weights_ref[...], preferred_element_type=jnp.float32)
+    out_ref[...] = total.astype(jnp.bfloat16)
+
+
+def place_halves(own_ref, other_ref, out_ref):
+    half = own_ref.shape[0]
+    core = lax.axis_index("c")
+    out_ref[pl.ds(pl.multiple_of(core * half, half), half), :] = own_ref[...]
+    out_ref[pl.ds(pl.multiple_of((1 - core) * half, half), half), :] = other_ref[...]
 
 
 def sum_and_cut(parts_ref, out_ref):
@@ -213,6 +236,7 @@
         scratch=[pltpu.VMEM((8,) + drafts.shape, drafts.dtype), pltpu.SemaphoreType.DMA((N_T // 8,))],
     )
     gathered = lax.all_to_all(copies, ("z", "yl"), 0, 0, tiled=True).reshape(rows, depth)
+    columns = down_codes.shape[1]
     weights = call(
         dequantize_pair,
         "dequantize_pair",
@@ -221,10 +245,12 @@
         3_000_000,
     )
     other_weights = lax.ppermute(weights, "c", CORES)
+    down = call(dequantize_one, "dequantize_one", down_codes.shape, (down_codes, down_scales), 1_000_000)
+    other_down = lax.ppermute(down, "c", CORES)
     flops = 2 * half * depth * width
-    theirs = call(take_theirs, "take_theirs", (half, depth), (gathered,), 1_000)
+    theirs = call(take_theirs, "take_theirs", (half, depth), (other_down[:16, :LANES], gathered), 1_000)
     other_rows = lax.ppermute(theirs, "c", CORES)
-    part, other_weights = call(
+    part, other_pair = call(
         times_own,
         "times_own",
         [((half, width), jnp.float32), ((depth, width), jnp.bfloat16)],
@@ -233,7 +259,7 @@
         specs=[pl.ANY, pltpu.VMEM, pltpu.VMEM, pltpu.HBM],
         scratch=[pltpu.SemaphoreType.DMA((4,))],
     )
-    sums = call(add_other, "add_other", (half, width), (part, other_rows, other_weights), flops)
+    sums = call(add_other, "add_other", (half, width), (part, other_rows, other_pair), flops)
     sums = lax.all_to_all(sums.reshape(4, half // 4, width), "x", 0, 0, tiled=True)
     pieces = call(sum_and_cut, "sum_and_cut", (4 * GROUPS, 24, LANES), (sums,), 1_000_000)
     pieces = lax.all_to_all(pieces, everyone, 0, 0, tiled=True)
@@ -245,16 +271,28 @@
         join_and_mix, "join_and_mix", (4, half // 4, UNITS), (pieces, jnp.asarray(block_matrix())), 200_000_000
     )
     rotated = lax.all_to_all(rotated, "x", 0, 0, tiled=True).reshape(half, UNITS)
-    other = lax.ppermute(rotated, "c", CORES)
-    down_weights = dequantize(down_codes, down_scales)
-    own_part = jnp.dot(rotated, down_weights, preferred_element_type=jnp.float32)
-    other_part = jnp.dot(other, down_weights, preferred_element_type=jnp.float32)
-    own_part, other_part = own_part.astype(jnp.bfloat16), other_part.astype(jnp.bfloat16)
-    partial_value = jnp.zeros((rows, own_part.shape[1]), jnp.bfloat16)
-    partial_value = lax.dynamic_update_slice_in_dim(partial_value, own_part, core * half, 0)
-    partial_value = lax.dynamic_update_slice_in_dim(partial_value, other_part, (1 - core) * half, 0)
+    flops = 2 * half * UNITS * columns
+    places = [pl.ANY, pltpu.VMEM, pltpu.VMEM]
+    sent = call(
+        times_down,
+        "their_columns",
+        (half, columns),
+        (rotated, rotated, other_down),
+        flops,
+        specs=places,
+    )
+    received = lax.ppermute(sent, "c", CORES)
+    kept = call(
+        times_down,
+        "our_columns",
+        (half, columns),
+        (sent, rotated, down),
+        flops,
+        specs=places,
+    )
+    partial_value = call(place_halves, "place_halves", (rows, columns), (kept, received), 1_000)
     partial_value = lax.all_to_all(
-        partial_value.reshape(N_T, rows // N_T, own_part.shape[1]), ("z", "yl"), 0, 0, tiled=True
+        partial_value.reshape(N_T, rows // N_T, columns), ("z", "yl"), 0, 0, tiled=True
     )
     return jnp.sum(partial_value.astype(jnp.float32), axis=0).astype(jnp.bfloat16)
 

time: 154 us -> 154 us (level)
  waiting for transfers between devices: 18.5 us -> 14.8 us
  starting transfers between devices: 19.6 us -> 22 us
    all_to_all x1, waiting for transfers between devices: 17.2 us -> 11.2 us  [per_device(): lax.all_to_all(copies, ('z', 'yl'), 0, 0, tiled=True).reshape(rows, depth)]
    ppermute x1 -> x2, starting transfers between devices: 1.91 us -> 4.33 us  [the longest x1 2.41 us: per_device(): other_down = lax.ppermute(down, 'c', CORES)]
    ppermute x1 -> x2, waiting for transfers between devices: 1.26 us -> 3.58 us  [the longest x1 2.47 us: per_device(): other_down = lax.ppermute(down, 'c', CORES)]
    pallas_call x8 -> x12, Pallas kernels: 5.16 us -> 6.52 us  [call(): pl.pallas_call(kernel, out_shape=shapes, in_specs=[whole(place) for place...]
    unnamed x16 -> x20, local copies, waits for them, and re-layouts: 2.72 us -> 3.66 us
  transfers between devices with their start and end apart: 4 -> 5, of which waited for: 2 -> 3; matrix products, arithmetic and copies ran while one was open for 1% -> 0% of each run, Pallas kernels for 1% -> 2%
where the time goes in v4:
time: 154 us; the launch traced here: 153 us
  blocking collectives  105 us (68%)
  starting transfers between devices  22 us (14%)
  waiting for transfers between devices  14.8 us (10%)
  Pallas kernels  6.52 us (4%)
  local copies, waits for them, and re-layouts  3.66 us (2%)
    all_to_all x1, blocking collectives, per_device(): lax.all_to_all(partial_value.reshape(N_T, rows // N_T, columns), ('z', 'y...  28.5 us
    all_to_all x1, blocking collectives, per_device(): pieces = lax.all_to_all(pieces, everyone, 0, 0, tiled=True)  23.7 us
    all_to_all x1, blocking collectives, per_device(): lax.all_to_all(sums.reshape(4, half // 4, width), 'x', 0, 0, tiled=True)  23.4 us
    all_to_all x1, blocking collectives, per_device(): lax.all_to_all(pieces.reshape(2 * N_T, 16, LANES), everyone, 0, 0, tiled=...  18.2 us
    all_to_all x1, starting transfers between devices, per_device(): lax.all_to_all(copies, ('z', 'yl'), 0, 0, tiled=True).reshape(rows, depth)  13.9 us
    all_to_all x1, blocking collectives, per_device(): lax.all_to_all(rotated, 'x', 0, 0, tiled=True).reshape(half, UNITS)  11.3 us
    all_to_all x1, waiting for transfers between devices, per_device(): lax.all_to_all(copies, ('z', 'yl'), 0, 0, tiled=True).reshape(rows, depth)  11.2 us
    pallas_call x12, Pallas kernels, call(): pl.pallas_call(kernel, out_shape=shapes, in_specs=[whole(place) for place...  6.52 us
  transfers between devices with their start and end apart: 5, of which 3 were waited for; matrix products, arithmetic and copies ran while one was open for 0% of the time, Pallas kernels for 2%

profile of v4, /device:TPU:16, one launch (start us, length us, event | category | flops | bytes accessed | tf_op | source)
XLA Modules:
  0.0 153.0 jit_solution(14917179773316368517)
XLA Ops:
  0.0 0.0 copy-start.4
  0.0 0.0 copy-start.6
  0.0 0.8 copy-done.6
  0.8 0.0 copy-start.8
  0.8 0.9 copy_out.1
  1.8 13.9 %all-to-all-start = ((bf16[32,24,512]{2,1,0:T(8,128)(2,1)}), bf16[32,24,512]{2,1,0:T(8,128)(2,1)S(1)}, u32[]{:S(2)}, u32[]{:S(2)}) async-start(bf16[32,24,512]{2,1,0:T(8,128)(2,1)} %copy_out.1), calls=%async_computation | async-start | bytes 1572864 | tf_op jit(solution)/shard_map/all_to_all | solution.py:238
  15.6 0.0 copy-done.4
  15.6 0.0 copy-done.8
  15.7 0.0 copy-start.5
  15.7 1.2 copy-done.5
  16.8 0.0 copy-start.9
  16.8 0.7 copy-done.9
  17.5 0.0 copy-start.3
  17.6 0.0 copy-start.7
  17.6 0.3 dequantize_pair.1.weights_ref
  17.9 1.9 %collective-permute-start.1 = (bf16[512,1792]{1,0:T(8,128)(2,1)S(1)}, bf16[512,1792]{1,0:T(8,128)(2,1)}, u32[]{:S(2)}, u32[]{:S(2)}) collective-permute-start(bf16[512,1792]{1,0:T(8,128)(2,1)S(1)} %dequantize_pair.1.weights_ref), channel_id=1, source_target_pairs={{0,32},{32,0},{1,33},{33,1},{2,34},{34,2},{3,35},{35,3},{4,36},{36... | collective-permute-start | bytes 5505032 | tf_op jit(solution)/shard_map/ppermute | solution.py:247
  19.8 0.0 copy-done.3
  19.8 0.0 copy-done.7
  19.8 0.2 dequantize_one.1.weights_ref
  20.0 2.4 %collective-permute-start = (bf16[896,512]{1,0:T(8,128)(2,1)S(1)}, bf16[896,512]{1,0:T(8,128)(2,1)S(1)}, u32[]{:S(2)}, u32[]{:S(2)}) collective-permute-start(bf16[896,512]{1,0:T(8,128)(2,1)S(1)} %dequantize_one.1.weights_ref), channel_id=1, source_target_pairs={{0,32},{32,0},{1,33},{33,1},{2,34},{34,2},{3,35},{35,3},{4,36},{36... | collective-permute-start | bytes 2752520 | tf_op jit(solution)/shard_map/ppermute | solution.py:249
  22.4 2.5 %collective-permute-done.weights_ref = bf16[896,512]{1,0:T(8,128)(2,1)S(1)} collective-permute-done((bf16[896,512]{1,0:T(8,128)(2,1)S(1)}, bf16[896,512]{1,0:T(8,128)(2,1)S(1)}, u32[]{:S(2)}, u32[]{:S(2)}) %collective-permute-start) | collective-permute-done | bytes 917536 | tf_op jit(solution)/shard_map/ppermute | solution.py:249
  24.9 0.0 copy-start.1
  24.9 0.9 copy-done.1
  25.8 11.2 %all-to-all-done = bf16[32,24,512]{2,1,0:T(8,128)(2,1)S(1)} async-done(((bf16[32,24,512]{2,1,0:T(8,128)(2,1)}), bf16[32,24,512]{2,1,0:T(8,128)(2,1)S(1)}, u32[]{:S(2)}, u32[]{:S(2)}) %all-to-all-start) | async-done | bytes 786464 | tf_op jit(solution)/shard_map/all_to_all | solution.py:238
  37.1 1.9 %collective-permute-start.2 = (bf16[384,512]{1,0:T(8,128)(2,1)S(1)}, bf16[384,512]{1,0:T(8,128)(2,1)S(1)}, u32[]{:S(2)}, u32[]{:S(2)}) collective-permute-start(bf16[384,512]{1,0:T(8,128)(2,1)S(1)} %take_theirs.1.after_ref), channel_id=1, source_target_pairs={{0,32},{32,0},{1,33},{33,1},{2,34},{34,2},{3,35},{35,3},{4,36},{36... | collective-permute-start | bytes 1179656 | tf_op jit(solution)/shard_map/ppermute | solution.py:252
  39.0 0.0 collective-permute-done.1.other_ref
  39.0 1.9 %times_own.1 = (f32[384,1792]{1,0:T(8,128)S(1)}, bf16[512,1792]{1,0:T(8,128)(2,1)S(1)}) custom-call(bf16[384,512]{1,0:T(8,128)(2,1)S(1)} %take_theirs.1.after_ref, bf16[768,512]{1,0:T(8,128)(2,1)S(1)} %bitcast.10, bf16[512,1792]{1,0:T(8,128)(2,1)S(1)} %dequantize_pair.1.weights_ref, bf16[512,1792]{1,0:T(8,128)(2,1)} %collective-permute-done.1.other_ref), custom_call_target="tpu_custom_call" | custom-call | flops 704643072 | bytes 2000000 | tf_op jit(solution)/shard_map/times_own/pallas_call | solution.py:69
  40.9 0.0 collective-permute-done.2.rows_ref
  41.0 0.9 add_other.1
  41.9 23.4 %all_to_all.30.parts_ref = bf16[4,96,1792]{2,1,0:T(8,128)(2,1)S(1)} all-to-all(bf16[4,96,1792]{2,1,0:T(8,128)(2,1)S(1)} %bitcast.11), channel_id=1, replica_groups=mesh['yh'=2,'x'=4,'c'=2,'z'=8,'yl'=4] {'x'}, dimensions={0} | all-to-all | bytes 2752512 | tf_op jit(solution)/shard_map/all_to_all | solution.py:263
  65.2 0.0 copy-start
  65.2 0.4 sum_and_cut.1
  65.6 23.7 %all_to_all.31 = bf16[64,24,128]{2,1,0:T(8,128)(2,1)S(1)} all-to-all(bf16[64,24,128]{2,1,0:T(8,128)(2,1)S(1)} %sum_and_cut.1), channel_id=1, replica_groups=mesh['yh'=2,'x'=4,'c'=2,'z'=8,'yl'=4] {'z','yl','yh'}, dimensions={0} | all-to-all | bytes 786432 | tf_op jit(solution)/shard_map/all_to_all | solution.py:265
  89.3 0.3 gate_and_mix.1
  89.6 18.2 %all_to_all.32.pieces_ref = bf16[64,16,128]{2,1,0:T(8,128)(2,1)S(1)} all-to-all(bf16[64,16,128]{2,1,0:T(8,128)(2,1)S(1)} %bitcast.14), channel_id=1, replica_groups=mesh['yh'=2,'x'=4,'c'=2,'z'=8,'yl'=4] {'z','yl','yh'}, dimensions={0} | all-to-all | bytes 524288 | tf_op jit(solution)/shard_map/all_to_all | solution.py:269
  107.8 0.0 copy-done
  107.8 0.0 copy-start.2
  107.8 0.5 join_and_mix.1
  108.3 11.3 %all_to_all.33 = bf16[4,96,896]{2,1,0:T(8,128)(2,1)S(1)} all-to-all(bf16[4,96,896]{2,1,0:T(8,128)(2,1)S(1)} %join_and_mix.1), channel_id=1, replica_groups=mesh['yh'=2,'x'=4,'c'=2,'z'=8,'yl'=4] {'x'}, dimensions={0} | all-to-all | bytes 1376256 | tf_op jit(solution)/shard_map/all_to_all | solution.py:273
  119.6 0.0 copy-done.2
  119.6 0.6 their_columns.1.after_ref
  120.2 1.9 %collective-permute-start.3 = (bf16[384,512]{1,0:T(8,128)(2,1)S(1)}, bf16[384,512]{1,0:T(8,128)(2,1)S(1)}, u32[]{:S(2)}, u32[]{:S(2)}) collective-permute-start(bf16[384,512]{1,0:T(8,128)(2,1)S(1)} %their_columns.1.after_ref), channel_id=1, source_target_pairs={{0,32},{32,0},{1,33},{33,1},{2,34},{34,2},{3,35},{35,3},{4,36},{36... | collective-permute-start | bytes 1179656 | tf_op jit(solution)/shard_map/ppermute | solution.py:284
  122.1 0.6 our_columns.1.own_ref
  122.7 1.1 collective-permute-done.3.other_ref
  123.8 0.1 place_halves.1
  123.9 28.5 %all_to_all.34 = bf16[32,24,512]{2,1,0:T(8,128)(2,1)S(1)} all-to-all(bf16[32,24,512]{2,1,0:T(8,128)(2,1)S(1)} %bitcast.12), channel_id=1, replica_groups=mesh['yh'=2,'x'=4,'c'=2,'z'=8,'yl'=4] {'z','yl'}, dimensions={0} | all-to-all | bytes 1572864 | tf_op jit(solution)/shard_map/all_to_all | solution.py:294
  152.3 0.7 reduce_sum.12
  (2 shorter events, 0.0 us)
Async XLA Ops:
  0.0 15.6 %copy-start.4 = (bf16[512,896]{1,0:T(8,128)(2,1)S(1)}, bf16[512,896]{1,0:T(8,128)(2,1)}, u32[]{:S(2)}) copy-start(bf16[512,896]{1,0:T(8,128)(2,1)} %gate_ref.1) | copy-start | bytes 2752516
  0.0 0.8 copy-start.6
  0.8 14.8 %copy-start.8 = (f32[4,896]{1,0:T(4,128)S(1)}, f32[4,896]{1,0:T(4,128)}, u32[]{:S(2)}) copy-start(f32[4,896]{1,0:T(4,128)} %gate_scales_ref.1) | copy-start | bytes 43012
  1.8 35.3 %all-to-all-start = ((bf16[32,24,512]{2,1,0:T(8,128)(2,1)}), bf16[32,24,512]{2,1,0:T(8,128)(2,1)S(1)}, u32[]{:S(2)}, u32[]{:S(2)}) async-start(bf16[32,24,512]{2,1,0:T(8,128)(2,1)} %copy_out.1), calls=%async_computation | async-start | bytes 1572864 | tf_op jit(solution)/shard_map/all_to_all | solution.py:238
  15.7 1.2 copy-start.5
  16.8 0.7 copy-start.9
  17.5 2.2 %copy-start.3 = (bf16[896,512]{1,0:T(8,128)(2,1)S(1)}, bf16[896,512]{1,0:T(8,128)(2,1)}, u32[]{:S(2)}) copy-start(bf16[896,512]{1,0:T(8,128)(2,1)} %codes_ref.1) | copy-start | bytes 2752516
  17.6 2.3 %copy-start.7 = (f32[7,512]{1,0:T(8,128)S(1)}, f32[7,512]{1,0:T(8,128)}, u32[]{:S(2)}) copy-start(f32[7,512]{1,0:T(8,128)} %scales_ref.1) | copy-start | bytes 43012
  17.9 21.1 %collective-permute-start.1 = (bf16[512,1792]{1,0:T(8,128)(2,1)S(1)}, bf16[512,1792]{1,0:T(8,128)(2,1)}, u32[]{:S(2)}, u32[]{:S(2)}) collective-permute-start(bf16[512,1792]{1,0:T(8,128)(2,1)S(1)} %dequantize_pair.1.weights_ref), channel_id=1, source_target_pairs={{0,32},{32,0},{1,33},{33,1},{2,34},{34,2},{3,35},{35,3},{4,36},{36... | collective-permute-start | bytes 5505032 | tf_op jit(solution)/shard_map/ppermute | solution.py:247
  20.0 4.9 %collective-permute-start = (bf16[896,512]{1,0:T(8,128)(2,1)S(1)}, bf16[896,512]{1,0:T(8,128)(2,1)S(1)}, u32[]{:S(2)}, u32[]{:S(2)}) collective-permute-start(bf16[896,512]{1,0:T(8,128)(2,1)S(1)} %dequantize_one.1.weights_ref), channel_id=1, source_target_pairs={{0,32},{32,0},{1,33},{33,1},{2,34},{34,2},{3,35},{35,3},{4,36},{36... | collective-permute-start | bytes 2752520 | tf_op jit(solution)/shard_map/ppermute | solution.py:249
  24.9 0.9 copy-start.1
  37.1 3.9 %collective-permute-start.2 = (bf16[384,512]{1,0:T(8,128)(2,1)S(1)}, bf16[384,512]{1,0:T(8,128)(2,1)S(1)}, u32[]{:S(2)}, u32[]{:S(2)}) collective-permute-start(bf16[384,512]{1,0:T(8,128)(2,1)S(1)} %take_theirs.1.after_ref), channel_id=1, source_target_pairs={{0,32},{32,0},{1,33},{33,1},{2,34},{34,2},{3,35},{35,3},{4,36},{36... | collective-permute-start | bytes 1179656 | tf_op jit(solution)/shard_map/ppermute | solution.py:252
  65.2 42.6 %copy-start = (bf16[896,896]{1,0:T(8,128)(2,1)S(1)}, bf16[896,896]{1,0:T(8,128)(2,1)}, u32[]{:S(2)}) copy-start(bf16[896,896]{1,0:T(8,128)(2,1)} %constant.5.clone.matrix_ref) | copy-start | bytes 4816900
  107.8 11.8 %copy-start.2 = (bf16[896,512]{1,0:T(8,128)(2,1)S(1)}, bf16[896,512]{1,0:T(8,128)(2,1)}, u32[]{:S(2)}) copy-start(bf16[896,512]{1,0:T(8,128)(2,1)} %copy-done.1) | copy-start | bytes 2752516
  120.2 3.6 %collective-permute-start.3 = (bf16[384,512]{1,0:T(8,128)(2,1)S(1)}, bf16[384,512]{1,0:T(8,128)(2,1)S(1)}, u32[]{:S(2)}, u32[]{:S(2)}) collective-permute-start(bf16[384,512]{1,0:T(8,128)(2,1)S(1)} %their_columns.1.after_ref), channel_id=1, source_target_pairs={{0,32},{32,0},{1,33},{33,1},{2,34},{34,2},{3,35},{35,3},{4,36},{36... | collective-permute-start | bytes 1179656 | tf_op jit(solution)/shard_map/ppermute | solution.py:284

commit v5 on v4

--- a/solution.py
+++ b/solution.py
@@ -257,7 +257,7 @@
         (theirs, gathered, weights, other_weights),
         flops,
         specs=[pl.ANY, pltpu.VMEM, pltpu.VMEM, pltpu.HBM],
-        scratch=[pltpu.SemaphoreType.DMA((4,))],
+        scratch=[pltpu.SemaphoreType.DMA((16,))],
     )
     sums = call(add_other, "add_other", (half, width), (part, other_rows, other_pair), flops)
     sums = lax.all_to_all(sums.reshape(4, half // 4, width), "x", 0, 0, tiled=True)

time: 154 us -> 154 us (level)
  no operation moved by 1% of the time
where the time goes in v5:
time: 154 us; the launch traced here: 153 us
  blocking collectives  105 us (68%)
  starting transfers between devices  22 us (14%)
  waiting for transfers between devices  14.8 us (10%)
  Pallas kernels  6.77 us (4%)
  local copies, waits for them, and re-layouts  3.66 us (2%)
    all_to_all x1, blocking collectives, per_device(): lax.all_to_all(partial_value.reshape(N_T, rows // N_T, columns), ('z', 'y...  28.4 us
    all_to_all x1, blocking collectives, per_device(): pieces = lax.all_to_all(pieces, everyone, 0, 0, tiled=True)  23.7 us
    all_to_all x1, blocking collectives, per_device(): lax.all_to_all(sums.reshape(4, half // 4, width), 'x', 0, 0, tiled=True)  23.4 us
    all_to_all x1, blocking collectives, per_device(): lax.all_to_all(pieces.reshape(2 * N_T, 16, LANES), everyone, 0, 0, tiled=...  18.3 us
    all_to_all x1, starting transfers between devices, per_device(): lax.all_to_all(copies, ('z', 'yl'), 0, 0, tiled=True).reshape(rows, depth)  13.9 us
    all_to_all x1, blocking collectives, per_device(): lax.all_to_all(rotated, 'x', 0, 0, tiled=True).reshape(half, UNITS)  11.3 us
    all_to_all x1, waiting for transfers between devices, per_device(): lax.all_to_all(copies, ('z', 'yl'), 0, 0, tiled=True).reshape(rows, depth)  11.2 us
    pallas_call x12, Pallas kernels, call(): pl.pallas_call(kernel, out_shape=shapes, in_specs=[whole(place) for place...  6.77 us
  transfers between devices with their start and end apart: 5, of which 3 were waited for; matrix products, arithmetic and copies ran while one was open for 0% of the time, Pallas kernels for 2%

profile of v5, /device:TPU:16, one launch (start us, length us, event | category | flops | bytes accessed | tf_op | source)
XLA Modules:
  0.0 153.3 jit_solution(15798320500595154373)
XLA Ops:
  0.0 0.0 copy-start.4
  0.0 0.0 copy-start.6
  0.0 0.8 copy-done.6
  0.8 0.0 copy-start.8
  0.8 0.9 copy_out.1
  1.8 13.9 %all-to-all-start = ((bf16[32,24,512]{2,1,0:T(8,128)(2,1)}), bf16[32,24,512]{2,1,0:T(8,128)(2,1)S(1)}, u32[]{:S(2)}, u32[]{:S(2)}) async-start(bf16[32,24,512]{2,1,0:T(8,128)(2,1)} %copy_out.1), calls=%async_computation | async-start | bytes 1572864 | tf_op jit(solution)/shard_map/all_to_all | solution.py:238
  15.6 0.0 copy-done.4
  15.6 0.0 copy-done.8
  15.7 0.0 copy-start.5
  15.7 1.2 copy-done.5
  16.8 0.0 copy-start.9
  16.8 0.7 copy-done.9
  17.5 0.0 copy-start.3
  17.6 0.0 copy-start.7
  17.6 0.3 dequantize_pair.1.weights_ref
  17.9 1.9 %collective-permute-start.1 = (bf16[512,1792]{1,0:T(8,128)(2,1)S(1)}, bf16[512,1792]{1,0:T(8,128)(2,1)}, u32[]{:S(2)}, u32[]{:S(2)}) collective-permute-start(bf16[512,1792]{1,0:T(8,128)(2,1)S(1)} %dequantize_pair.1.weights_ref), channel_id=1, source_target_pairs={{0,32},{32,0},{1,33},{33,1},{2,34},{34,2},{3,35},{35,3},{4,36},{36... | collective-permute-start | bytes 5505032 | tf_op jit(solution)/shard_map/ppermute | solution.py:247
  19.8 0.0 copy-done.3
  19.8 0.0 copy-done.7
  19.8 0.2 dequantize_one.1.weights_ref
  20.0 2.4 %collective-permute-start = (bf16[896,512]{1,0:T(8,128)(2,1)S(1)}, bf16[896,512]{1,0:T(8,128)(2,1)S(1)}, u32[]{:S(2)}, u32[]{:S(2)}) collective-permute-start(bf16[896,512]{1,0:T(8,128)(2,1)S(1)} %dequantize_one.1.weights_ref), channel_id=1, source_target_pairs={{0,32},{32,0},{1,33},{33,1},{2,34},{34,2},{3,35},{35,3},{4,36},{36... | collective-permute-start | bytes 2752520 | tf_op jit(solution)/shard_map/ppermute | solution.py:249
  22.4 2.5 %collective-permute-done.weights_ref = bf16[896,512]{1,0:T(8,128)(2,1)S(1)} collective-permute-done((bf16[896,512]{1,0:T(8,128)(2,1)S(1)}, bf16[896,512]{1,0:T(8,128)(2,1)S(1)}, u32[]{:S(2)}, u32[]{:S(2)}) %collective-permute-start) | collective-permute-done | bytes 917536 | tf_op jit(solution)/shard_map/ppermute | solution.py:249
  24.9 0.0 copy-start.1
  24.9 0.9 copy-done.1
  25.8 11.2 %all-to-all-done = bf16[32,24,512]{2,1,0:T(8,128)(2,1)S(1)} async-done(((bf16[32,24,512]{2,1,0:T(8,128)(2,1)}), bf16[32,24,512]{2,1,0:T(8,128)(2,1)S(1)}, u32[]{:S(2)}, u32[]{:S(2)}) %all-to-all-start) | async-done | bytes 786464 | tf_op jit(solution)/shard_map/all_to_all | solution.py:238
  37.1 1.9 %collective-permute-start.2 = (bf16[384,512]{1,0:T(8,128)(2,1)S(1)}, bf16[384,512]{1,0:T(8,128)(2,1)S(1)}, u32[]{:S(2)}, u32[]{:S(2)}) collective-permute-start(bf16[384,512]{1,0:T(8,128)(2,1)S(1)} %take_theirs.1.after_ref), channel_id=1, source_target_pairs={{0,32},{32,0},{1,33},{33,1},{2,34},{34,2},{3,35},{35,3},{4,36},{36... | collective-permute-start | bytes 1179656 | tf_op jit(solution)/shard_map/ppermute | solution.py:252
  39.0 0.0 collective-permute-done.1.other_ref
  39.0 2.2 %times_own.1 = (f32[384,1792]{1,0:T(8,128)S(1)}, bf16[512,1792]{1,0:T(8,128)(2,1)S(1)}) custom-call(bf16[384,512]{1,0:T(8,128)(2,1)S(1)} %take_theirs.1.after_ref, bf16[768,512]{1,0:T(8,128)(2,1)S(1)} %bitcast.10, bf16[512,1792]{1,0:T(8,128)(2,1)S(1)} %dequantize_pair.1.weights_ref, bf16[512,1792]{1,0:T(8,128)(2,1)} %collective-permute-done.1.other_ref), custom_call_target="tpu_custom_call" | custom-call | flops 704643072 | bytes 2000000 | tf_op jit(solution)/shard_map/times_own/pallas_call | solution.py:69
  41.2 0.0 collective-permute-done.2.rows_ref
  41.2 0.9 add_other.1
  42.1 23.4 %all_to_all.30.parts_ref = bf16[4,96,1792]{2,1,0:T(8,128)(2,1)S(1)} all-to-all(bf16[4,96,1792]{2,1,0:T(8,128)(2,1)S(1)} %bitcast.11), channel_id=1, replica_groups=mesh['yh'=2,'x'=4,'c'=2,'z'=8,'yl'=4] {'x'}, dimensions={0} | all-to-all | bytes 2752512 | tf_op jit(solution)/shard_map/all_to_all | solution.py:263
  65.5 0.0 copy-start
  65.5 0.4 sum_and_cut.1
  65.8 23.7 %all_to_all.31 = bf16[64,24,128]{2,1,0:T(8,128)(2,1)S(1)} all-to-all(bf16[64,24,128]{2,1,0:T(8,128)(2,1)S(1)} %sum_and_cut.1), channel_id=1, replica_groups=mesh['yh'=2,'x'=4,'c'=2,'z'=8,'yl'=4] {'z','yl','yh'}, dimensions={0} | all-to-all | bytes 786432 | tf_op jit(solution)/shard_map/all_to_all | solution.py:265
  89.5 0.3 gate_and_mix.1
  89.8 18.3 %all_to_all.32.pieces_ref = bf16[64,16,128]{2,1,0:T(8,128)(2,1)S(1)} all-to-all(bf16[64,16,128]{2,1,0:T(8,128)(2,1)S(1)} %bitcast.14), channel_id=1, replica_groups=mesh['yh'=2,'x'=4,'c'=2,'z'=8,'yl'=4] {'z','yl','yh'}, dimensions={0} | all-to-all | bytes 524288 | tf_op jit(solution)/shard_map/all_to_all | solution.py:269
  108.1 0.0 copy-done
  108.1 0.0 copy-start.2
  108.1 0.5 join_and_mix.1
  108.5 11.3 %all_to_all.33 = bf16[4,96,896]{2,1,0:T(8,128)(2,1)S(1)} all-to-all(bf16[4,96,896]{2,1,0:T(8,128)(2,1)S(1)} %join_and_mix.1), channel_id=1, replica_groups=mesh['yh'=2,'x'=4,'c'=2,'z'=8,'yl'=4] {'x'}, dimensions={0} | all-to-all | bytes 1376256 | tf_op jit(solution)/shard_map/all_to_all | solution.py:273
  119.9 0.0 copy-done.2
  119.9 0.6 their_columns.1.after_ref
  120.4 1.9 %collective-permute-start.3 = (bf16[384,512]{1,0:T(8,128)(2,1)S(1)}, bf16[384,512]{1,0:T(8,128)(2,1)S(1)}, u32[]{:S(2)}, u32[]{:S(2)}) collective-permute-start(bf16[384,512]{1,0:T(8,128)(2,1)S(1)} %their_columns.1.after_ref), channel_id=1, source_target_pairs={{0,32},{32,0},{1,33},{33,1},{2,34},{34,2},{3,35},{35,3},{4,36},{36... | collective-permute-start | bytes 1179656 | tf_op jit(solution)/shard_map/ppermute | solution.py:284
  122.4 0.6 our_columns.1.own_ref
  123.0 1.1 collective-permute-done.3.other_ref
  124.1 0.1 place_halves.1
  124.1 28.4 %all_to_all.34 = bf16[32,24,512]{2,1,0:T(8,128)(2,1)S(1)} all-to-all(bf16[32,24,512]{2,1,0:T(8,128)(2,1)S(1)} %bitcast.12), channel_id=1, replica_groups=mesh['yh'=2,'x'=4,'c'=2,'z'=8,'yl'=4] {'z','yl'}, dimensions={0} | all-to-all | bytes 1572864 | tf_op jit(solution)/shard_map/all_to_all | solution.py:294
  152.6 0.7 reduce_sum.12
  (2 shorter events, 0.0 us)
Async XLA Ops:
  0.0 15.6 %copy-start.4 = (bf16[512,896]{1,0:T(8,128)(2,1)S(1)}, bf16[512,896]{1,0:T(8,128)(2,1)}, u32[]{:S(2)}) copy-start(bf16[512,896]{1,0:T(8,128)(2,1)} %gate_ref.1) | copy-start | bytes 2752516
  0.0 0.8 copy-start.6
  0.8 14.8 %copy-start.8 = (f32[4,896]{1,0:T(4,128)S(1)}, f32[4,896]{1,0:T(4,128)}, u32[]{:S(2)}) copy-start(f32[4,896]{1,0:T(4,128)} %gate_scales_ref.1) | copy-start | bytes 43012
  1.8 35.3 %all-to-all-start = ((bf16[32,24,512]{2,1,0:T(8,128)(2,1)}), bf16[32,24,512]{2,1,0:T(8,128)(2,1)S(1)}, u32[]{:S(2)}, u32[]{:S(2)}) async-start(bf16[32,24,512]{2,1,0:T(8,128)(2,1)} %copy_out.1), calls=%async_computation | async-start | bytes 1572864 | tf_op jit(solution)/shard_map/all_to_all | solution.py:238
  15.7 1.2 copy-start.5
  16.8 0.7 copy-start.9
  17.5 2.2 %copy-start.3 = (bf16[896,512]{1,0:T(8,128)(2,1)S(1)}, bf16[896,512]{1,0:T(8,128)(2,1)}, u32[]{:S(2)}) copy-start(bf16[896,512]{1,0:T(8,128)(2,1)} %codes_ref.1) | copy-start | bytes 2752516
  17.6 2.3 %copy-start.7 = (f32[7,512]{1,0:T(8,128)S(1)}, f32[7,512]{1,0:T(8,128)}, u32[]{:S(2)}) copy-start(f32[7,512]{1,0:T(8,128)} %scales_ref.1) | copy-start | bytes 43012
  17.9 21.1 %collective-permute-start.1 = (bf16[512,1792]{1,0:T(8,128)(2,1)S(1)}, bf16[512,1792]{1,0:T(8,128)(2,1)}, u32[]{:S(2)}, u32[]{:S(2)}) collective-permute-start(bf16[512,1792]{1,0:T(8,128)(2,1)S(1)} %dequantize_pair.1.weights_ref), channel_id=1, source_target_pairs={{0,32},{32,0},{1,33},{33,1},{2,34},{34,2},{3,35},{35,3},{4,36},{36... | collective-permute-start | bytes 5505032 | tf_op jit(solution)/shard_map/ppermute | solution.py:247
  20.0 4.9 %collective-permute-start = (bf16[896,512]{1,0:T(8,128)(2,1)S(1)}, bf16[896,512]{1,0:T(8,128)(2,1)S(1)}, u32[]{:S(2)}, u32[]{:S(2)}) collective-permute-start(bf16[896,512]{1,0:T(8,128)(2,1)S(1)} %dequantize_one.1.weights_ref), channel_id=1, source_target_pairs={{0,32},{32,0},{1,33},{33,1},{2,34},{34,2},{3,35},{35,3},{4,36},{36... | collective-permute-start | bytes 2752520 | tf_op jit(solution)/shard_map/ppermute | solution.py:249
  24.9 0.9 copy-start.1
  37.1 4.1 %collective-permute-start.2 = (bf16[384,512]{1,0:T(8,128)(2,1)S(1)}, bf16[384,512]{1,0:T(8,128)(2,1)S(1)}, u32[]{:S(2)}, u32[]{:S(2)}) collective-permute-start(bf16[384,512]{1,0:T(8,128)(2,1)S(1)} %take_theirs.1.after_ref), channel_id=1, source_target_pairs={{0,32},{32,0},{1,33},{33,1},{2,34},{34,2},{3,35},{35,3},{4,36},{36... | collective-permute-start | bytes 1179656 | tf_op jit(solution)/shard_map/ppermute | solution.py:252
  65.5 42.6 %copy-start = (bf16[896,896]{1,0:T(8,128)(2,1)S(1)}, bf16[896,896]{1,0:T(8,128)(2,1)}, u32[]{:S(2)}) copy-start(bf16[896,896]{1,0:T(8,128)(2,1)} %constant.5.clone.matrix_ref) | copy-start | bytes 4816900
  108.1 11.8 %copy-start.2 = (bf16[896,512]{1,0:T(8,128)(2,1)S(1)}, bf16[896,512]{1,0:T(8,128)(2,1)}, u32[]{:S(2)}) copy-start(bf16[896,512]{1,0:T(8,128)(2,1)} %copy-done.1) | copy-start | bytes 2752516
  120.4 3.6 %collective-permute-start.3 = (bf16[384,512]{1,0:T(8,128)(2,1)S(1)}, bf16[384,512]{1,0:T(8,128)(2,1)S(1)}, u32[]{:S(2)}, u32[]{:S(2)}) collective-permute-start(bf16[384,512]{1,0:T(8,128)(2,1)S(1)} %their_columns.1.after_ref), channel_id=1, source_target_pairs={{0,32},{32,0},{1,33},{33,1},{2,34},{34,2},{3,35},{35,3},{4,36},{36... | collective-permute-start | bytes 1179656 | tf_op jit(solution)/shard_map/ppermute | solution.py:284
